TPU v7x, 128 devices: a whole 4x4x4 slice. The times are simulated.
128 devices in a mesh: ctx: 32 (over z, y, x_hi), exp: 4 (over x_lo, core).
Axes of the slice: x: 4 (x_hi: 2, x_lo: 2; x = x_hi * 2 + x_lo), y: 4, z: 4, core: 2. Of those that a mesh axis runs over, the one named last changes fastest.
Arguments:
- residual_in: bfloat16 [4096, 3072], P('ctx', 'exp'), may hold values from -6 to 6
- residual_tan: bfloat16 [4096, 3072], P('ctx', 'exp'), may hold values from -6 to 6
- queries: bfloat16 [4096, 1536], P('ctx', 'exp'), may hold values from -96 to 96
- keys: bfloat16 [4096, 1536], P('ctx', 'exp'), may hold values from -4 to 4
- values: bfloat16 [4096, 1536], P('ctx', 'exp'), may hold values from -6 to 6
- query_tan: bfloat16 [4096, 1536], P('ctx', 'exp'), may hold values from -6 to 6
- key_tan: bfloat16 [4096, 1536], P('ctx', 'exp'), may hold values from -6 to 6
- value_tan: bfloat16 [4096, 1536], P('ctx', 'exp'), may hold values from -6 to 6
- out_proj: bfloat16 [1536, 3072], P('exp'), may hold values from -0.15625 to 0.15625
- shift_mod: float32 [3072], replicated, may hold values from -3 to 3
- scale_mod: float32 [3072], replicated, may hold values from -1.5 to 1.5
- router: bfloat16 [3072, 16], replicated, may hold values from -0.109375 to 0.109375
- up_weight: bfloat16 [32, 3072, 6144], P('ctx', None, 'exp'), may hold values from -0.109375 to 0.109375
- down_weight: bfloat16 [32, 6144, 3072], P('ctx', 'exp'), may hold values from -0.0546875 to 0.0546875
- expert_ids: int32 [4096, 2], P('ctx'), may hold values from 0 to 15, all different within a row; in each aligned block of 128 rows (0 to 127, 128 to 255, ...) at most 20 rows name the same one
Outputs:
- mixed: bfloat16 [4096, 3072], P('ctx', 'exp')
- mixed_tan: bfloat16 [4096, 3072], P('ctx', 'exp')
Inputs may be any that keep to these rules, and one draw needn't show every extreme that they name: `expert_ids`: each row names two different experts. Among the 128 rows of one ctx index no expert is named more than 20 times, and in some such block one expert is named exactly 20 times; every expert is named by some row.
All inputs are finite; a program needn't handle non-finite values.
Results may differ from a plain program's by a relative error of at most 0.018.
Values may be sent and summed in bfloat16 or wider, within the bound.
A program may use at most 192 MiB of HBM per device.

v0:
```python
import jax
import jax.numpy as jnp
from jax import lax
from jax.sharding import PartitionSpec as P

D = 3072
HD = 128


EPS = 1e-06


def gelu_tanh(inputs):
    return jax.nn.gelu(inputs, approximate=True)


def modulate(state_f, tan_f, meansq, cross, shift_part, scale_part):
    recip = lax.rsqrt(meansq + EPS)
    unit = state_f * recip
    unit_tan = tan_f * recip - state_f * (recip * recip * recip) * cross
    normed = (unit * (1.0 + scale_part) + shift_part).astype(jnp.bfloat16)
    normed_tan = (unit_tan * (1.0 + scale_part)).astype(jnp.bfloat16)
    return (normed, normed_tan)


def gating(logits, logit_tan, expert_ids):
    picker = (
        expert_ids[:, :, None] == jnp.arange(logits.shape[1], dtype=jnp.int32)[None, None, :]
    ).astype(jnp.float32)
    own = jnp.sum(picker * logits[:, None, :], axis=2)
    own_tan = jnp.sum(picker * logit_tan[:, None, :], axis=2)
    other = own[:, ::-1]
    other_tan = own_tan[:, ::-1]
    gates = 1.0 / (1.0 + jnp.exp(other - own))
    gates_tan = gates * (1.0 - gates) * (own_tan - other_tan)
    return (gates, gates_tan)


def slot_targets(block_ids, experts, capacity):
    flat_ids = block_ids.reshape(-1)
    onehot = (flat_ids[:, None] == jnp.arange(experts, dtype=jnp.int32)[None, :]).astype(jnp.int32)
    ranks = jnp.cumsum(onehot, axis=0) - onehot
    within = jnp.sum(ranks * onehot, axis=1)
    return flat_ids * capacity + within


def shards(
    residual_in,
    residual_tan,
    queries,
    keys,
    values,
    query_tan,
    key_tan,
    value_tan,
    out_proj,
    shift_mod,
    scale_mod,
    router,
    up_weight,
    down_weight,
    expert_ids,
):
    tok_rows = queries.shape[0]
    heads_here = queries.shape[1] // HD
    factor = HD ** (-0.5)

    def to_heads(block):
        return block.reshape(block.shape[0], heads_here, HD)

    q_heads = to_heads(queries)
    qt_heads = to_heads(query_tan)
    highest = jnp.full((heads_here, tok_rows), -1e30, jnp.float32)
    key_piece = lax.all_gather(keys, "ctx", axis=0, tiled=True)
    value_piece = lax.all_gather(values, "ctx", axis=0, tiled=True)
    ktan_piece = lax.all_gather(key_tan, "ctx", axis=0, tiled=True)
    vtan_piece = lax.all_gather(value_tan, "ctx", axis=0, tiled=True)
    key_heads = to_heads(key_piece)
    ktan_heads = to_heads(ktan_piece)
    value_heads = to_heads(value_piece)
    vtan_heads = to_heads(vtan_piece)
    scores = (
        jnp.einsum("thd,phd->htp", q_heads, key_heads, preferred_element_type=jnp.float32) * factor
    )
    score_tan = (
        jnp.einsum("thd,phd->htp", qt_heads, key_heads, preferred_element_type=jnp.float32)
        + jnp.einsum("thd,phd->htp", q_heads, ktan_heads, preferred_element_type=jnp.float32)
    ) * factor
    new_high = jnp.maximum(highest, jnp.max(scores, axis=2))
    weights = jnp.exp(scores - new_high[:, :, None])
    tilted = weights * score_tan
    denominator = jnp.sum(weights, axis=2)
    mass = jnp.sum(tilted, axis=2)
    weights_b = weights.astype(jnp.bfloat16)
    tilted_b = tilted.astype(jnp.bfloat16)
    accum = jnp.einsum("htp,phd->htd", weights_b, value_heads, preferred_element_type=jnp.float32)
    taccum = jnp.einsum(
        "htp,phd->htd", tilted_b, value_heads, preferred_element_type=jnp.float32
    ) + jnp.einsum("htp,phd->htd", weights_b, vtan_heads, preferred_element_type=jnp.float32)
    highest, denominator, mass, accum, taccum = (new_high, denominator, mass, accum, taccum)
    head_out = accum / denominator[:, :, None]
    head_tan = taccum / denominator[:, :, None] - head_out * (mass / denominator)[:, :, None]
    attended = head_out.transpose(1, 0, 2).reshape(tok_rows, heads_here * HD).astype(jnp.bfloat16)
    attended_tan = (
        head_tan.transpose(1, 0, 2).reshape(tok_rows, heads_here * HD).astype(jnp.bfloat16)
    )
    projected = jnp.dot(attended, out_proj, preferred_element_type=jnp.float32)
    projected_tan = jnp.dot(attended_tan, out_proj, preferred_element_type=jnp.float32)
    summed, summed_tan = (
        lax.psum_scatter(
            projected.astype(jnp.bfloat16), "exp", scatter_dimension=1, tiled=True
        ).astype(jnp.float32),
        lax.psum_scatter(
            projected_tan.astype(jnp.bfloat16), "exp", scatter_dimension=1, tiled=True
        ).astype(jnp.float32),
    )
    state = (residual_in.astype(jnp.float32) + summed).astype(jnp.bfloat16)
    state_tan = (residual_tan.astype(jnp.float32) + summed_tan).astype(jnp.bfloat16)
    whole, whole_tan = (
        lax.all_gather(state, "exp", axis=1, tiled=True),
        lax.all_gather(state_tan, "exp", axis=1, tiled=True),
    )
    whole_f = whole.astype(jnp.float32)
    wtan_f = whole_tan.astype(jnp.float32)
    meansq = jnp.mean(whole_f * whole_f, axis=1, keepdims=True)
    cross = jnp.mean(whole_f * wtan_f, axis=1, keepdims=True)
    normed, normed_tan = modulate(whole_f, wtan_f, meansq, cross, shift_mod, scale_mod)
    logits = jnp.dot(normed, router, preferred_element_type=jnp.float32)
    logit_tan = jnp.dot(normed_tan, router, preferred_element_type=jnp.float32)
    gates, gates_tan = gating(logits, logit_tan, expert_ids)
    experts = router.shape[1]
    capacity = 5 * tok_rows // (2 * experts)
    ctx_count = lax.axis_size("ctx")
    rows_dev = up_weight.shape[0]
    pieces = rows_dev * ctx_count // experts
    targets = slot_targets(expert_ids, experts, capacity)
    matches = (
        targets.reshape(tok_rows, 2)[:, :, None]
        == jnp.arange(experts * capacity, dtype=jnp.int32)[None, None, :]
    )
    select = jnp.sum(matches.astype(jnp.bfloat16), axis=1)
    packed = jnp.einsum("ts,td->sd", select, normed, preferred_element_type=jnp.float32).astype(
        jnp.bfloat16
    )
    packed_tan = jnp.einsum(
        "ts,td->sd", select, normed_tan, preferred_element_type=jnp.float32
    ).astype(jnp.bfloat16)
    packed = jnp.broadcast_to(
        packed.reshape(experts, 1, capacity, D), (experts, pieces, capacity, D)
    ).reshape(experts * pieces, capacity, D)
    packed_tan = jnp.broadcast_to(
        packed_tan.reshape(experts, 1, capacity, D), (experts, pieces, capacity, D)
    ).reshape(experts * pieces, capacity, D)
    rows_in, rows_tan = (
        lax.all_to_all(packed, "ctx", split_axis=0, concat_axis=1, tiled=True),
        lax.all_to_all(packed_tan, "ctx", split_axis=0, concat_axis=1, tiled=True),
    )
    pre = jnp.einsum("rmd,rdf->rmf", rows_in, up_weight, preferred_element_type=jnp.float32)
    pre_tan = jnp.einsum("rmd,rdf->rmf", rows_tan, up_weight, preferred_element_type=jnp.float32)
    act, act_tan = jax.jvp(gelu_tanh, (pre,), (pre_tan,))
    expert_out = jnp.einsum(
        "rmf,rfd->rmd", act.astype(jnp.bfloat16), down_weight, preferred_element_type=jnp.float32
    ).astype(jnp.bfloat16)
    expert_tan = jnp.einsum(
        "rmf,rfd->rmd",
        act_tan.astype(jnp.bfloat16),
        down_weight,
        preferred_element_type=jnp.float32,
    ).astype(jnp.bfloat16)
    expert_out = expert_out.reshape(rows_dev, ctx_count, capacity, D)
    expert_tan = expert_tan.reshape(rows_dev, ctx_count, capacity, D)
    back_rows, back_tan = (
        lax.all_to_all(expert_out, "ctx", split_axis=1, concat_axis=0, tiled=True),
        lax.all_to_all(expert_tan, "ctx", split_axis=1, concat_axis=0, tiled=True),
    )
    folded = jnp.sum(back_rows.reshape(experts, pieces, capacity, D).astype(jnp.float32), axis=1)
    folded_tan = jnp.sum(back_tan.reshape(experts, pieces, capacity, D).astype(jnp.float32), axis=1)
    picked = folded.reshape(experts * capacity, D)[targets].reshape(tok_rows, 2, D)
    picked_tan = folded_tan.reshape(experts * capacity, D)[targets].reshape(tok_rows, 2, D)
    moe = jnp.sum(gates[:, :, None] * picked, axis=1)
    moe_tan = jnp.sum(gates_tan[:, :, None] * picked + gates[:, :, None] * picked_tan, axis=1)
    moe_part, moe_tan_part = (
        lax.psum_scatter(moe.astype(jnp.bfloat16), "exp", scatter_dimension=1, tiled=True).astype(
            jnp.float32
        ),
        lax.psum_scatter(
            moe_tan.astype(jnp.bfloat16), "exp", scatter_dimension=1, tiled=True
        ).astype(jnp.float32),
    )
    mixed = (state.astype(jnp.float32) + moe_part).astype(jnp.bfloat16)
    mixed_tan = (state_tan.astype(jnp.float32) + moe_tan_part).astype(jnp.bfloat16)
    return (mixed, mixed_tan)


def solution(mesh):
    in_specs = (
        P("ctx", "exp"),
        P("ctx", "exp"),
        P("ctx", "exp"),
        P("ctx", "exp"),
        P("ctx", "exp"),
        P("ctx", "exp"),
        P("ctx", "exp"),
        P("ctx", "exp"),
        P("exp", None),
        P(),
        P(),
        P(),
        P("ctx", None, "exp"),
        P("ctx", "exp", None),
        P("ctx", None),
    )
    out_specs = (P("ctx", "exp"), P("ctx", "exp"))
    return jax.shard_map(shards, mesh=mesh, in_specs=in_specs, out_specs=out_specs, check_vma=False)
```

profile of v0, /device:TPU:0, one launch (start us, length us, event | category | flops | bytes accessed | tf_op | source)
XLA Modules:
  0.0 830.3 jit_solution(5223690270095372566)
XLA Ops:
  14.0 74.7 %all-gather.11.cloned.1.call-done = bf16[4096,384]{1,0:T(8,128)(2,1)} async-done(((bf16[128,384]{1,0:T(8,128)(2,1)}), bf16[4096,384]{1,0:T(8,128)(2,1)}) %all-gather.11.cloned.1.call-update) | async-done | bytes 3145744 | tf_op jit(solution)/shard_map/all_gather | solution.py:77
  93.4 79.9 %all-gather.5.cloned.1.call-done = bf16[4096,384]{0,1:T(8,128)(2,1)} async-done(((bf16[128,384]{0,1:T(8,128)(2,1)}), bf16[4096,384]{0,1:T(8,128)(2,1)}) %all-gather.5.cloned.1.call-update) | async-done | bytes 3145744 | tf_op jit(solution)/shard_map/all_gather | solution.py:74
  184.2 72.6 %all-gather.9.cloned.1.call-done = bf16[4096,384]{0,1:T(8,128)(2,1)} async-done(((bf16[128,384]{0,1:T(8,128)(2,1)}), bf16[4096,384]{0,1:T(8,128)(2,1)}) %all-gather.9.cloned.1.call-update) | async-done | bytes 3145744 | tf_op jit(solution)/shard_map/all_gather | solution.py:76
  256.8 9.5 %fusion.94 = (f32[3,128]{1,0:T(4,128)S(1)}, bf16[3,128,4096]{2,1,0:T(8,128)(2,1)}) fusion(f32[3,128,4096]{2,1,0:T(8,128)} %fusion.95, bf16[128,3,128]{0,2,1:T(8,128)(2,1)S(1)} %bitcast.104, bf16[4096,3,128]{0,2,1:T(8,128)(2,1)} %bitcast.102, f32[3,128,4096]{2,1,0:T(8,128)} %copy-done.2, f32[3,128]{1,0:T(4,128)S(1)} %broadcast_maximum_fusion), kind=kOutput, calls=%fused_computation.118 | convolution fusion | flops 412089984 | bytes 18975744 | tf_op jit(solution)/shard_map/thd,phd->htp/dot_general | solution.py:87
  267.5 65.2 %all-gather.7.cloned.1.call-done = bf16[4096,384]{1,0:T(8,128)(2,1)} async-done(((bf16[128,384]{1,0:T(8,128)(2,1)}), bf16[4096,384]{1,0:T(8,128)(2,1)}) %all-gather.7.cloned.1.call-update) | async-done | bytes 3145744 | tf_op jit(solution)/shard_map/all_gather | solution.py:75
  349.0 14.9 %reduce-scatter.9.cloned.1.call-done = bf16[128,768]{1,0:T(8,128)(2,1)} async-done(((bf16[128,3072]{1,0:T(8,128)(2,1)}), bf16[128,768]{1,0:T(8,128)(2,1)}) %reduce-scatter.9.cloned.1.call-update) | async-done | bytes 196624 | tf_op jit(solution)/shard_map/reduce_scatter | solution.py:113
  364.8 8.8 %all_gather.23 = bf16[128,3072]{1,0:T(8,128)(2,1)S(1)} all-gather(bf16[128,768]{1,0:T(8,128)(2,1)S(1)} %add_convert_fusion.1), channel_id=1, replica_groups=mesh['ctx'=32,'exp'=4] {'exp'}, dimensions={1}, use_global_device_ids=true | all-gather | bytes 983040 | tf_op jit(solution)/shard_map/all_gather | solution.py:121
  373.6 12.5 %reduce-scatter.5.cloned.1.call-done = bf16[128,768]{1,0:T(8,128)(2,1)} async-done(((bf16[128,3072]{1,0:T(8,128)(2,1)}), bf16[128,768]{1,0:T(8,128)(2,1)}) %reduce-scatter.5.cloned.1.call-update) | async-done | bytes 196624 | tf_op jit(solution)/shard_map/reduce_scatter | solution.py:110
  387.2 9.0 %all_gather.20 = bf16[128,3072]{1,0:T(8,128)(2,1)S(1)} all-gather(bf16[128,768]{1,0:T(8,128)(2,1)S(1)} %add_convert_fusion.3), channel_id=1, replica_groups=mesh['ctx'=32,'exp'=4] {'exp'}, dimensions={1}, use_global_device_ids=true | all-gather | bytes 983040 | tf_op jit(solution)/shard_map/all_gather | solution.py:120
  407.0 9.4 %all-to-all-start = ((bf16[32,20,3072]{2,1,0:T(8,128)(2,1)}), bf16[32,20,3072]{2,1,0:T(8,128)(2,1)}, u32[]{:S(2)}, u32[]{:S(2)}) async-start(bf16[32,20,3072]{2,1,0:T(8,128)(2,1)} %bitcast.94), calls=%async_computation.1 | async-start | bytes 9437184 | tf_op jit(solution)/shard_map/all_to_all | solution.py:155
  422.8 58.1 %all-to-all-done = bf16[32,20,3072]{2,1,0:T(8,128)(2,1)} async-done(((bf16[32,20,3072]{2,1,0:T(8,128)(2,1)}), bf16[32,20,3072]{2,1,0:T(8,128)(2,1)}, u32[]{:S(2)}, u32[]{:S(2)}) %all-to-all-start) | async-done | bytes 3932192 | tf_op jit(solution)/shard_map/all_to_all | solution.py:155
  485.5 15.3 %all-to-all-start.2 = ((bf16[32,20,3072]{2,1,0:T(8,128)(2,1)}), bf16[32,20,3072]{2,1,0:T(8,128)(2,1)}, u32[]{:S(2)}, u32[]{:S(2)}) async-start(bf16[32,20,3072]{2,1,0:T(8,128)(2,1)} %bitcast.95), calls=%async_computation.5 | async-start | bytes 9437184 | tf_op jit(solution)/shard_map/all_to_all | solution.py:156
  507.7 11.3 %fusion.6 = f32[640,1536]{1,0:T(8,128)} fusion(bf16[640,3072]{1,0:T(8,128)(2,1)} %reshape.216, bf16[1,3072,1536]{2,1,0:T(8,128)(2,1)} %param.27), kind=kOutput, calls=%fused_computation.10 | convolution fusion | flops 6039797760 | bytes 17301504 | tf_op jit(solution)/shard_map/rmd,rdf->rmf/dot_general | solution.py:158
  519.0 40.1 %all-to-all-done.2 = bf16[32,20,3072]{2,1,0:T(8,128)(2,1)} async-done(((bf16[32,20,3072]{2,1,0:T(8,128)(2,1)}), bf16[32,20,3072]{2,1,0:T(8,128)(2,1)}, u32[]{:S(2)}, u32[]{:S(2)}) %all-to-all-start.2) | async-done | bytes 3932192 | tf_op jit(solution)/shard_map/all_to_all | solution.py:156
  559.1 6.9 reshape.226
  566.0 23.0 %fusion.13 = bf16[640,3072]{1,0:T(8,128)(2,1)} fusion(bf16[1,1536,3072]{2,1,0:T(8,128)(2,1)} %param.28, f32[640,1536]{1,0:T(8,128)} %fusion.6, bf16[640,3072]{1,0:T(8,128)(2,1)} %reshape.226, bf16[1,3072,1536]{2,1,0:T(8,128)(2,1)} %param.27), kind=kOutput, calls=%fused_computation.20 | convolution fusion | flops 12101222400 | bytes 30670848 | tf_op jit(solution)/shard_map/rmf,rfd->rmd/dot_general | solution.py:164
  595.8 10.3 %all-to-all-start.3 = ((bf16[1,32,20,3072]{3,2,0,1:T(8,128)(2,1)}), bf16[1,32,20,3072]{3,2,0,1:T(8,128)(2,1)}, u32[]{:S(2)}, u32[]{:S(2)}) async-start(bf16[1,32,20,3072]{3,2,0,1:T(8,128)(2,1)} %bitcast.96), calls=%async_computation.6 | async-start | bytes 9437184 | tf_op jit(solution)/shard_map/all_to_all | solution.py:174
  606.2 11.8 %fusion.10 = bf16[640,3072]{1,0:T(8,128)(2,1)} fusion(bf16[1,1536,3072]{2,1,0:T(8,128)(2,1)} %param.28, f32[640,1536]{1,0:T(8,128)} %fusion.6), kind=kOutput, calls=%fused_computation.19 | convolution fusion | flops 6050611200 | bytes 17301504 | tf_op jit(solution)/shard_map/rmf,rfd->rmd/dot_general | solution.py:161
  624.8 41.5 %all-to-all-done.3 = bf16[1,32,20,3072]{3,2,0,1:T(8,128)(2,1)} async-done(((bf16[1,32,20,3072]{3,2,0,1:T(8,128)(2,1)}), bf16[1,32,20,3072]{3,2,0,1:T(8,128)(2,1)}, u32[]{:S(2)}, u32[]{:S(2)}) %all-to-all-start.3) | async-done | bytes 3932192 | tf_op jit(solution)/shard_map/all_to_all | solution.py:174
  666.3 12.1 %all-to-all-start.1 = ((bf16[1,32,20,3072]{3,2,0,1:T(8,128)(2,1)}), bf16[1,32,20,3072]{3,2,0,1:T(8,128)(2,1)}, u32[]{:S(2)}, u32[]{:S(2)}) async-start(bf16[1,32,20,3072]{3,2,0,1:T(8,128)(2,1)} %bitcast.93), calls=%async_computation.2 | async-start | bytes 9437184 | tf_op jit(solution)/shard_map/all_to_all | solution.py:173
  702.6 33.9 %all-to-all-done.1 = bf16[1,32,20,3072]{3,2,0,1:T(8,128)(2,1)} async-done(((bf16[1,32,20,3072]{3,2,0,1:T(8,128)(2,1)}), bf16[1,32,20,3072]{3,2,0,1:T(8,128)(2,1)}, u32[]{:S(2)}, u32[]{:S(2)}) %all-to-all-start.1) | async-done | bytes 3932192 | tf_op jit(solution)/shard_map/all_to_all | solution.py:173
  759.4 13.8 %add_reduce_fusion = (bf16[128,3072]{1,0:T(8,128)(2,1)}, bf16[128,3072]{1,0:T(8,128)(2,1)}) fusion(f32[128,2,3072]{2,1,0:T(2,128)} %reshape.229, f32[128,2,3072]{2,1,0:T(2,128)} %reshape.221, f32[128,2]{1,0:T(8,128)S(1)} %copy.85, f32[128,2]{1,0:T(8,128)S(1)} %copy.71), kind=kLoop, calls=%fused_computation.39 | loop fusion | flops 3932160 | bytes 7866368 | tf_op jit(solution)/shard_map/reduce_sum | solution.py:181
  773.9 24.9 %reduce-scatter.11.cloned.1.call-done = bf16[128,768]{1,0:T(8,128)(2,1)} async-done(((bf16[128,3072]{1,0:T(8,128)(2,1)}), bf16[128,768]{1,0:T(8,128)(2,1)}) %reduce-scatter.11.cloned.1.call-update) | async-done | bytes 196624 | tf_op jit(solution)/shard_map/reduce_scatter | solution.py:186
  800.5 20.9 %reduce-scatter.7.cloned.1.call-done = bf16[128,768]{1,0:T(8,128)(2,1)} async-done(((bf16[128,3072]{1,0:T(8,128)(2,1)}), bf16[128,768]{1,0:T(8,128)(2,1)}) %reduce-scatter.7.cloned.1.call-update) | async-done | bytes 196624 | tf_op jit(solution)/shard_map/reduce_scatter | solution.py:183
  (109 shorter events, 134.9 us)
Async XLA Ops:
  7.2 337.0 %copy-start = (bf16[384,3072]{1,0:T(8,128)(2,1)S(1)}, bf16[384,3072]{1,0:T(8,128)(2,1)}, u32[]{:S(2)}) copy-start(bf16[384,3072]{1,0:T(8,128)(2,1)} %param.23) | copy-start | bytes 7077892
  7.2 81.5 %all-gather.11.cloned.1.call-start = ((), (), s32[]{:S(2)}) async-start(), calls=%async_computation.13 | async-start | bytes 3244032 | tf_op jit(solution)/shard_map/all_gather | solution.py:77
  7.9 165.4 %all-gather.5.cloned.1.call-start = ((), (), s32[]{:S(2)}) async-start(), calls=%async_computation.8 | async-start | bytes 3244032 | tf_op jit(solution)/shard_map/all_gather | solution.py:74
  9.6 247.2 %all-gather.9.cloned.1.call-start = ((), (), s32[]{:S(2)}) async-start(), calls=%async_computation.12 | async-start | bytes 3244032 | tf_op jit(solution)/shard_map/all_gather | solution.py:76
  11.3 321.4 %all-gather.7.cloned.1.call-start = ((), (), s32[]{:S(2)}) async-start(), calls=%async_computation.9 | async-start | bytes 3244032 | tf_op jit(solution)/shard_map/all_gather | solution.py:75
  11.9 351.9 %reduce-scatter.9.cloned.1.call-start = ((), (), s32[]{:S(2)}) async-start(), calls=%async_computation.14 | async-start | bytes 983040 | tf_op jit(solution)/shard_map/reduce_scatter | solution.py:113
  176.4 4.2 copy-start.6
  256.8 9.5 %copy-start.3 = (f32[3,128,4096]{2,1,0:T(8,128)S(1)}, f32[3,128,4096]{2,1,0:T(8,128)}, u32[]{:S(2)}) copy-start(f32[3,128,4096]{2,1,0:T(8,128)} %copy-done.2) | copy-start | bytes 18874372
  256.8 9.5 %copy-start.4 = (bf16[4096,384]{0,1:T(8,128)(2,1)S(1)}, bf16[4096,384]{0,1:T(8,128)(2,1)}, u32[]{:S(2)}) copy-start(bf16[4096,384]{0,1:T(8,128)(2,1)} %copy.84) | copy-start | bytes 9437188
  337.6 5.0 copy-start.5
  337.6 5.6 copy-start.7
  344.2 4.8 copy-start.12
  344.2 19.7 %copy-start.8 = (bf16[128,768]{1,0:T(8,128)(2,1)S(1)}, bf16[128,768]{1,0:T(8,128)(2,1)}, u32[]{:S(2)}) copy-start(bf16[128,768]{1,0:T(8,128)(2,1)} %param.16) | copy-start | bytes 589828
  345.7 40.5 %copy-start.9 = (bf16[128,768]{1,0:T(8,128)(2,1)S(1)}, bf16[128,768]{1,0:T(8,128)(2,1)}, u32[]{:S(2)}) copy-start(bf16[128,768]{1,0:T(8,128)(2,1)} %param.15) | copy-start | bytes 589828
  345.8 40.4 %reduce-scatter.5.cloned.1.call-start = ((), (), s32[]{:S(2)}) async-start(), calls=%async_computation.10 | async-start | bytes 983040 | tf_op jit(solution)/shard_map/reduce_scatter | solution.py:110
  347.3 49.3 %copy-start.11 = (f32[3072]{0:T(1024)S(1)}, f32[3072]{0:T(1024)}, u32[]{:S(2)}) copy-start(f32[3072]{0:T(1024)} %param.24) | copy-start | bytes 36868
  407.0 74.0 %all-to-all-start = ((bf16[32,20,3072]{2,1,0:T(8,128)(2,1)}), bf16[32,20,3072]{2,1,0:T(8,128)(2,1)}, u32[]{:S(2)}, u32[]{:S(2)}) async-start(bf16[32,20,3072]{2,1,0:T(8,128)(2,1)} %bitcast.94), calls=%async_computation.1 | async-start | bytes 9437184 | tf_op jit(solution)/shard_map/all_to_all | solution.py:155
  485.5 73.6 %all-to-all-start.2 = ((bf16[32,20,3072]{2,1,0:T(8,128)(2,1)}), bf16[32,20,3072]{2,1,0:T(8,128)(2,1)}, u32[]{:S(2)}, u32[]{:S(2)}) async-start(bf16[32,20,3072]{2,1,0:T(8,128)(2,1)} %bitcast.95), calls=%async_computation.5 | async-start | bytes 9437184 | tf_op jit(solution)/shard_map/all_to_all | solution.py:156
  595.8 70.5 %all-to-all-start.3 = ((bf16[1,32,20,3072]{3,2,0,1:T(8,128)(2,1)}), bf16[1,32,20,3072]{3,2,0,1:T(8,128)(2,1)}, u32[]{:S(2)}, u32[]{:S(2)}) async-start(bf16[1,32,20,3072]{3,2,0,1:T(8,128)(2,1)} %bitcast.96), calls=%async_computation.6 | async-start | bytes 9437184 | tf_op jit(solution)/shard_map/all_to_all | solution.py:174
  666.3 12.5 %copy-start.10 = (bf16[3072,16]{0,1:T(8,128)(2,1)S(1)}, bf16[3072,16]{0,1:T(8,128)(2,1)}, u32[]{:S(2)}) copy-start(bf16[3072,16]{0,1:T(8,128)(2,1)} %param.26) | copy-start | bytes 294916
  666.3 70.2 %all-to-all-start.1 = ((bf16[1,32,20,3072]{3,2,0,1:T(8,128)(2,1)}), bf16[1,32,20,3072]{3,2,0,1:T(8,128)(2,1)}, u32[]{:S(2)}, u32[]{:S(2)}) async-start(bf16[1,32,20,3072]{3,2,0,1:T(8,128)(2,1)} %bitcast.93), calls=%async_computation.2 | async-start | bytes 9437184 | tf_op jit(solution)/shard_map/all_to_all | solution.py:173
  678.4 120.4 %reduce-scatter.11.cloned.1.call-start = ((), (), s32[]{:S(2)}) async-start(), calls=%async_computation.15 | async-start | bytes 983040 | tf_op jit(solution)/shard_map/reduce_scatter | solution.py:186
  754.2 68.9 %copy-start.1 = (bf16[384,3072]{1,0:T(8,128)(2,1)S(1)}, bf16[384,3072]{1,0:T(8,128)(2,1)}, u32[]{:S(2)}) copy-start(bf16[384,3072]{1,0:T(8,128)(2,1)} %param.23) | copy-start | bytes 7077892
  773.2 48.2 %reduce-scatter.7.cloned.1.call-start = ((), (), s32[]{:S(2)}) async-start(), calls=%async_computation.11 | async-start | bytes 983040 | tf_op jit(solution)/shard_map/reduce_scatter | solution.py:183
  (2 other events, 6.3 us)
Sparse Core Ops, SparseCore 0:
  11.0 77.6 all-gather.10
  92.0 81.2 all-gather.4
  176.6 80.1 all-gather.8
  259.7 73.0 all-gather.6
  345.9 17.9 reduce-scatter.8
  366.1 20.0 reduce-scatter.4
  773.3 25.4 reduce-scatter.10
  801.2 20.0 reduce-scatter.6
where the time goes:
time: 842 us; the launch traced here: 830 us
  waiting for transfers between devices  541 us (64%)
  local copies, waits for them, and re-layouts  97.7 us (12%)
  matrix products  77.2 us (9%)
  starting transfers between devices  47.7 us (6%)
  other arithmetic  33.8 us (4%)
  blocking collectives  17.8 us (2%)
  between operations  14.9 us (2%)
    all_gather x1, waiting for transfers between devices, shards(): key_piece = lax.all_gather(keys, 'ctx', axis=0, tiled=True)  79.9 us
    all_gather x1, waiting for transfers between devices, shards(): vtan_piece = lax.all_gather(value_tan, 'ctx', axis=0, tiled=True)  74.7 us
    all_gather x1, waiting for transfers between devices, shards(): ktan_piece = lax.all_gather(key_tan, 'ctx', axis=0, tiled=True)  72.6 us
    all_gather x1, waiting for transfers between devices, shards(): value_piece = lax.all_gather(values, 'ctx', axis=0, tiled=True)  65.2 us
    all_to_all x1, waiting for transfers between devices, shards(): lax.all_to_all(packed, 'ctx', split_axis=0, concat_axis=1, tiled=True)  58.1 us
    all_to_all x1, waiting for transfers between devices, shards(): lax.all_to_all(expert_tan, 'ctx', split_axis=1, concat_axis=0, tiled=True)  41.5 us
    all_to_all x1, waiting for transfers between devices, shards(): lax.all_to_all(packed_tan, 'ctx', split_axis=0, concat_axis=1, tiled=True)  40.1 us
    all_to_all x1, waiting for transfers between devices, shards(): lax.all_to_all(expert_out, 'ctx', split_axis=1, concat_axis=0, tiled=True)  33.9 us
  transfers between devices with their start and end apart: 12, of which 12 were waited for; matrix products, arithmetic and copies ran while one was open for 12% of the time, Pallas kernels for 0%

commit v1 on v0

v1 whole, which is shorter than its diff:
```python
import functools

import jax
import jax.numpy as jnp
import numpy as np
from jax import lax
from jax.experimental import pallas as pl
from jax.experimental.pallas import tpu as pltpu
from jax.sharding import PartitionSpec as P

D = 3072
HD = 128
TOK = 128
HEADS_HERE = 3
WIDTH = HEADS_HERE * HD
QUARTER = 768
EXPERTS = 16
CAP = 20
USED = 2 * CAP
SLAB = 48
PAIR = 2 * USED
ROWS = 640
HALF = ROWS // 2
HIDDEN = 1536
EPS = 1e-06
FACTOR = HD ** (-0.5)
LOG2E = 1.4426950408889634
MIB = 2**20

BF = jnp.bfloat16
F32 = jnp.float32
MESH = pl.DeviceIdType.MESH
VMEM = pltpu.VMEM
NT = (((1,), (1,)), ((), ()))
TN = (((0,), (0,)), ((), ()))
NN = (((1,), (0,)), ((), ()))


def dot(a, b, dims=NN):
    return lax.dot_general(a, b, dims, preferred_element_type=F32)


def coords():
    c = lax.axis_index("ctx")
    e = lax.axis_index("exp")
    return c // 8, (c // 2) % 4, c % 2, e // 2, e % 2


def device(z, y, xh, xl, core):
    return (z * 8 + y * 2 + xh, xl * 2 + core)


def meet(peers):
    barrier = pltpu.get_barrier_semaphore()
    for peer in peers:
        pl.semaphore_signal(barrier, inc=1, device_id=peer, device_id_type=MESH)
    pl.semaphore_wait(barrier, len(peers))


def remote(src, dst, send, recv, peer):
    return pltpu.make_async_remote_copy(
        src_ref=src, dst_ref=dst, send_sem=send, recv_sem=recv, device_id=peer, device_id_type=MESH
    )


YX = [(a, b) for a in range(4) for b in range(2) if a or b]
ZY = [(a, b) for a in range(4) for b in range(4) if a or b]


def gather_kernel(q, qt, k, v, kt, vt, qg, qtg, kg, vg, ktg, vtg, ssem, rsem, lsem):
    z, y, xh, xl, co = coords()
    here = y * 2 + xh
    peers_z = [device((z + a) % 4, y, xh, xl, co) for a in (1, 3, 2)]
    peers_q = [device(z, (y + a) % 4, (xh + b) % 2, xl, co) for a, b in YX]
    meet(peers_z + peers_q)
    copies = []
    n = 0
    for peer in peers_z:
        for src, dst in ((k, kg), (kt, ktg), (v, vg), (vt, vtg)):
            copies.append(remote(src, dst.at[z], ssem.at[n], rsem.at[n], peer))
            copies[-1].start()
            n += 1
    for peer in peers_q:
        for src, dst in ((q, qg), (qt, qtg)):
            copies.append(remote(src, dst.at[here], ssem.at[n], rsem.at[n], peer))
            copies[-1].start()
            n += 1
    own = ((k, kg, z), (kt, ktg, z), (v, vg, z), (vt, vtg, z), (q, qg, here), (qt, qtg, here))
    for i, (src, dst, at) in enumerate(own):
        copies.append(pltpu.make_async_copy(src, dst.at[at], lsem.at[i]))
        copies[-1].start()
    for copy in copies:
        copy.wait()


def attend_kernel(q, qt, k, kt, v, vt, out, stats):
    rows = []
    for h in range(HEADS_HERE):
        c = slice(h * HD, (h + 1) * HD)
        qh, qth = q[:, :, c].reshape(256, HD), qt[:, :, c].reshape(256, HD)
        kh, kth = k[:, :, c].reshape(512, HD), kt[:, :, c].reshape(512, HD)
        vh, vth = v[:, :, c].reshape(512, HD), vt[:, :, c].reshape(512, HD)
        scores = dot(kh, qh, NT) * (FACTOR * LOG2E)
        tan = dot(jnp.concatenate([kh, kth], 1), jnp.concatenate([qth, qh], 1), NT) * FACTOR
        high = jnp.max(scores, axis=0, keepdims=True)
        weights = jnp.exp2(scores - high)
        total = jnp.sum(weights, axis=0, keepdims=True)
        weights = weights * (1.0 / total)
        mean = jnp.sum(weights * tan, axis=0, keepdims=True)
        tilted = (weights * (tan - mean)).astype(BF)
        both = dot(weights.astype(BF), jnp.concatenate([vh, vth], 1), TN)
        tout = both[:, HD:] + dot(tilted, vh, TN)
        out[:, :, c] = both[:, :HD].astype(BF).reshape(2, TOK, HD)
        out[:, :, WIDTH + h * HD : WIDTH + (h + 1) * HD] = tout.astype(BF).reshape(2, TOK, HD)
        rows.append((high + jnp.log2(total), mean))
    pad = jnp.zeros((2, 256), F32)
    table = jnp.concatenate([r[0] for r in rows] + [r[1] for r in rows] + [pad], axis=0)
    stats[0] = table[:, :TOK]
    stats[1] = table[:, TOK:]


def spread_tables():
    col = np.arange(EXPERTS * SLAB)
    row = col % SLAB
    slot = np.where(row < 16, row, np.where(row < 32, row - 16, np.where(row < 36, row - 16, row - 20)))
    slot = np.where(row < USED, slot, -1)
    tan = ((row >= 16) & (row < 32)) | ((row >= 36) & (row < USED))
    spread = (np.arange(EXPERTS)[:, None] == (col // SLAB)[None, :]).astype(np.float32)
    info = np.zeros((8, EXPERTS * SLAB), np.float32)
    info[0] = np.where(tan, -1, slot)
    info[1] = np.where(tan, slot, -1)
    return spread, info


def to_columns(rows):
    n = rows.shape[0]
    return jnp.concatenate([rows, jnp.zeros((128 - n, 128), F32)], axis=0).T


def middle_kernel(
    ot, stats, out_proj, res, rest, shift, scale, router, ids, spread, info,
    packed, state, ghi, glo,
    got, gstats, mine, sib, far, farin, mstat, gstat, mlog, glog, acc,
    s1, r1, s2, r2, s3, r3, s4, r4, s5, r5, lsem,
):
    z, y, xh, xl, co = coords()
    e = xl * 2 + co
    here = y * 2 + xh
    sibling = device(z, y, xh, xl, 1 - co)
    across = device(z, y, xh, 1 - xl, co)
    diagonal = device(z, y, xh, 1 - xl, 1 - co)
    peers_q = [device(z, (y + a) % 4, (xh + b) % 2, xl, co) for a, b in YX]
    peers_e = [sibling, across, diagonal]
    meet(peers_q + peers_e)
    first = []
    for n, ((a, b), peer) in enumerate(zip(YX, peers_q)):
        there = ((y + a) % 4) * 2 + (xh + b) % 2
        first.append(remote(stats.at[there], gstats.at[here], s2.at[n], r2.at[n], peer))
        first[-1].start()
        first.append(remote(ot.at[there], got.at[here], s1.at[n], r1.at[n], peer))
        first[-1].start()
    for i, (src, dst) in enumerate(((stats, gstats), (ot, got))):
        first.append(pltpu.make_async_copy(src.at[here], dst.at[here], lsem.at[i]))
        first[-1].start()

    expert = lax.broadcasted_iota(jnp.int32, (EXPERTS, TOK), 0)
    oh0 = (ids[0:1, :] == expert).astype(F32)
    oh1 = (ids[1:2, :] == expert).astype(F32)
    named = oh0 + oh1
    before = (
        lax.broadcasted_iota(jnp.int32, (TOK, TOK), 0) < lax.broadcasted_iota(jnp.int32, (TOK, TOK), 1)
    ).astype(BF)
    rank = dot(named.astype(BF), before)
    spread_b = spread[...]
    named_x = dot(named.astype(BF), spread_b, TN)
    rank_x = dot(rank.astype(BF), spread_b, TN)
    sel = jnp.where(rank_x == info[0:1, :], named_x, 0.0)
    selt = jnp.where(rank_x == info[1:2, :], named_x, 0.0)
    select = jnp.concatenate([sel, selt], axis=0).astype(BF)

    for copy in first:
        copy.wait()

    lse = [gstats[j, 0:3, :] for j in range(8)]
    mean = [gstats[j, 3:6, :] for j in range(8)]
    top = functools.reduce(jnp.maximum, lse)
    part = [jnp.exp2(item - top) for item in lse]
    inv = 1.0 / functools.reduce(jnp.add, part)
    part = [item * inv for item in part]
    mid = functools.reduce(jnp.add, [p * m for p, m in zip(part, mean)])
    lean = [p * (m - mid) for p, m in zip(part, mean)]
    cols = to_columns(jnp.concatenate(part + lean, axis=0))
    for h in range(HEADS_HERE):
        o = jnp.zeros((TOK, HD), F32)
        t = jnp.zeros((TOK, HD), F32)
        for j in range(8):
            oj = got[j, :, h * HD : (h + 1) * HD].astype(F32)
            tj = got[j, :, WIDTH + h * HD : WIDTH + (h + 1) * HD].astype(F32)
            w = cols[:, j * 3 + h : j * 3 + h + 1]
            c = cols[:, 24 + j * 3 + h : 24 + j * 3 + h + 1]
            o = o + w * oj
            t = t + w * tj + c * oj
        acc[0:TOK, h * HD : (h + 1) * HD] = o.astype(BF)
        acc[TOK:, h * HD : (h + 1) * HD] = t.astype(BF)

    att = acc[...]

    def project(xl_to, core_to):
        at = pl.multiple_of((xl_to * 2 + core_to) * QUARTER, QUARTER)
        return dot(att, out_proj[:, pl.ds(at, QUARTER)])

    mine[0] = project(1 - xl, 1 - co).astype(BF)
    to_sib0 = remote(mine.at[0], sib.at[0], s3.at[0], r3.at[0], sibling)
    to_sib0.start()
    mine[1] = project(xl, 1 - co).astype(BF)
    to_sib1 = remote(mine.at[1], sib.at[1], s3.at[1], r3.at[1], sibling)
    to_sib1.start()
    away = project(1 - xl, co)
    to_sib0.wait()
    far[...] = (away + sib[0].astype(F32)).astype(BF)
    to_far = remote(far, farin, s3.at[2], r3.at[2], across)
    to_far.start()
    kept = project(xl, co)
    to_sib1.wait()
    kept = kept + sib[1].astype(F32)
    to_far.wait()
    kept = kept + farin[...].astype(F32)
    st = (res[...].astype(F32) + kept[:TOK]).astype(BF)
    stt = (rest[...].astype(F32) + kept[TOK:]).astype(BF)
    state[0:TOK] = st
    state[TOK:] = stt
    sf = st.astype(F32)
    tf = stt.astype(F32)

    lane = lax.broadcasted_iota(jnp.int32, (TOK, 128), 1)
    sq = jnp.sum(sf * sf, axis=1, keepdims=True)
    cr = jnp.sum(sf * tf, axis=1, keepdims=True)
    mstat[...] = jnp.where(lane == 0, sq, jnp.where(lane == 1, cr, 0.0)).T[0:8]
    sends = []
    for n, peer in enumerate(peers_e):
        sends.append(remote(mstat, gstat.at[n], s4.at[n], r4.at[n], peer))
        sends[-1].start()
    for copy in sends:
        copy.wait()
    both = to_columns((mstat[...] + gstat[0]) + (gstat[1] + gstat[2])) * (1.0 / D)
    meansq, cross = both[:, 0:1], both[:, 1:2]
    recip = lax.rsqrt(meansq + EPS)
    gain = 1.0 + scale[pl.ds(e, 1), :]
    normed = (sf * recip * gain + shift[pl.ds(e, 1), :]).astype(BF)
    normed_tan = ((tf * recip - sf * (recip * recip * recip) * cross) * gain).astype(BF)
    rows = jnp.concatenate([normed, normed_tan], axis=0)

    mlog[...] = dot(router[e], rows, NT)
    sends = []
    for n, peer in enumerate(peers_e):
        sends.append(remote(mlog, glog.at[n], s5.at[n], r5.at[n], peer))
        sends[-1].start()
    for i in range(4):
        at = slice(i * 192, (i + 1) * 192)
        packed[i * 4 : (i + 1) * 4] = dot(select[:, at], rows, TN).astype(BF).reshape(4, SLAB, QUARTER)
    for copy in sends:
        copy.wait()

    logits = (mlog[...] + glog[0]) + (glog[1] + glog[2])
    ll, lt = logits[:, :TOK], logits[:, TOK:]
    own0 = jnp.sum(oh0 * ll, axis=0, keepdims=True)
    own1 = jnp.sum(oh1 * ll, axis=0, keepdims=True)
    diff = jnp.sum(oh0 * lt, axis=0, keepdims=True) - jnp.sum(oh1 * lt, axis=0, keepdims=True)
    gate0 = 1.0 / (1.0 + jnp.exp(own1 - own0))
    gate1 = 1.0 / (1.0 + jnp.exp(own0 - own1))
    gates = oh0 * gate0 + oh1 * gate1
    gates_tan = oh0 * (gate0 * (1.0 - gate0) * diff) - oh1 * (gate1 * (1.0 - gate1) * diff)
    ghigh = gates.astype(BF)
    glow = (gates - ghigh.astype(F32)).astype(BF)
    thigh = gates_tan.astype(BF)
    tlow = (gates_tan - thigh.astype(F32)).astype(BF)
    for ref, g, t in ((ghi, ghigh, thigh), (glo, glow, tlow)):
        gx = dot(g, spread_b, TN)
        tx = dot(t, spread_b, TN)
        ref[0:TOK] = (sel * gx).astype(BF)
        ref[TOK:] = (sel * tx + selt * gx).astype(BF)


def gelu_rows(v):
    n = v.shape[1]
    v = v.reshape(16, USED, n)
    p, t = v[:, 0:16].reshape(256, n), v[:, 16:32].reshape(256, n)
    mix = v[:, 32:40].reshape(128, n)
    low = lax.broadcasted_iota(jnp.int32, (128, n), 0) % 8 < 4
    u = jnp.where(low, mix, pltpu.roll(mix, 4, 0))

    def curves(x):
        sq = x * x
        th = jnp.tanh(0.7978845608028654 * x * (1.0 + 0.044715 * sq))
        half = 0.5 * (1.0 + th)
        slope = half + 0.5 * x * (1.0 - th * th) * (0.7978845608028654 * (1.0 + 0.134145 * sq))
        return x * half, slope

    g, s = curves(p)
    gm, sm = curves(u)
    m = jnp.where(low, gm, sm * mix)
    out = jnp.concatenate(
        [g.reshape(16, 16, n), (s * t).reshape(16, 16, n), m.reshape(16, 8, n)], axis=1
    )
    return out.reshape(ROWS, n).astype(BF)


def expert_kernel(
    packed, state, ghi, glo, up, down,
    mixed, mixed_tan,
    upv, downv, zin, x, pre, act, sibin, fwd_l, fwd_r, fin_l, fin_r, zout, zback,
    wsem, s1, r1, s2, r2, s3, r3, s4, r4, lsem,
):
    z, y, xh, xl, co = coords()
    pos = xh * 2 + xl
    here = z * 4 + y
    right, left, off = (pos + 1) % 4, (pos + 3) % 4, (pos + 2) % 4
    pair, other = xh * 2 + 1 - xl, (1 - xh) * 2 + 1 - xl

    def at_pos(p, c):
        return device(z, y, p // 2, p % 2, c)

    to_r, to_l, to_sib = at_pos(right, co), at_pos(left, co), at_pos(pos, 1 - co)
    peers = [device((z + a) % 4, (y + b) % 4, xh, xl, co) for a, b in ZY]
    load_up = pltpu.make_async_copy(up.at[0], upv, wsem.at[0])
    load_down = pltpu.make_async_copy(down.at[0], downv, wsem.at[1])
    meet(peers + [to_r, to_l, to_sib])

    moves = []
    for n, ((a, b), peer) in enumerate(zip(ZY, peers)):
        there = ((z + a) % 4) * 4 + (y + b) % 4
        moves.append(remote(packed.at[there], zin.at[here], s1.at[n], r1.at[n], peer))
        moves[-1].start()
    moves.append(pltpu.make_async_copy(packed.at[here], zin.at[here], lsem.at[0]))
    moves[-1].start()
    load_up.start()
    load_down.start()
    for copy in moves:
        copy.wait()
    block = pos * 2 + co

    def join(g, carry):
        a = zin[2 * g].astype(F32)[:USED]
        b = zin[2 * g + 1].astype(F32)[:USED]
        at = pl.multiple_of(g * PAIR, PAIR)
        x[block, pl.ds(at, PAIR), :] = jnp.concatenate([a, b], axis=0).astype(BF)
        return carry

    lax.fori_loop(0, 8, join, 0)

    def pass_on(n, b, half, peer):
        ref = x.at[b] if half is None else x.at[b, pl.ds(half * HALF, HALF)]
        return remote(ref, ref, s2.at[n], r2.at[n], peer)

    bl, br, bo = left * 2 + co, right * 2 + co, off * 2 + co
    c = [
        pass_on(0, block, None, to_sib),
        pass_on(1, block, 0, to_r),
        pass_on(2, block, 1, to_r),
        pass_on(3, block, 1, to_l),
        pass_on(4, block, 0, to_l),
        pass_on(5, bl, 0, to_r),
        pass_on(6, br, 1, to_l),
        pass_on(7, bl, 0, to_sib),
        pass_on(8, bl, 1, to_sib),
        pass_on(9, br, 0, to_sib),
        pass_on(10, br, 1, to_sib),
        pass_on(11, bo, 0, to_sib),
        pass_on(12, bo, 1, to_sib),
    ]
    for n in (1, 3, 0, 2, 4):
        c[n].start()

    def up_tile(p, n):
        cols = pl.ds(pl.multiple_of(n * 256, 256), 256)
        rows = pl.ds(pl.multiple_of((p % 2) * HIDDEN, HIDDEN), QUARTER)
        more = pl.ds(pl.multiple_of((p % 2) * HIDDEN + QUARTER, QUARTER), QUARTER)
        return dot(x[2 * p], upv[rows, cols]) + dot(x[2 * p + 1], upv[more, cols]), cols

    def up_first(p, at):
        def tile(n, carry):
            value, cols = up_tile(p, n)
            pre[at, :, cols] = value
            return carry

        lax.fori_loop(0, 6, tile, 0)

    def up_second(p, at):
        def tile(n, carry):
            value, cols = up_tile(p, n)
            act[at, :, cols] = gelu_rows(pre[at, :, cols] + value)
            return carry

        lax.fori_loop(0, 6, tile, 0)

    load_up.wait()
    c[0].wait_recv()
    up_first(pos, 0)
    c[1].wait_recv()
    c[5].start()
    c[7].start()
    c[3].wait_recv()
    c[6].start()
    c[10].start()
    c[2].wait_recv()
    c[8].start()
    c[4].wait_recv()
    c[9].start()
    for n in (7, 10, 8, 9):
        c[n].wait_recv()
    up_second(pair, 0)
    up_first(other, 1)
    c[5].wait_recv()
    c[11].start()
    c[6].wait_recv()
    c[12].start()
    c[11].wait_recv()
    c[12].wait_recv()
    up_second(off, 1)
    for copy in c:
        copy.wait_send()
    load_down.wait()

    def down_block(slot, p, core_to):
        at = jnp.where(p // 2 == xh, 0, 1)

        def tile(n, carry):
            first = ((p % 2) * 2 + core_to) * QUARTER
            cols = pl.ds(pl.multiple_of(first + n * 256, 256), 256)
            x[slot, :, pl.ds(pl.multiple_of(n * 256, 256), 256)] = dot(act[at], downv[:, cols]).astype(BF)
            return carry

        lax.fori_loop(0, 3, tile, 0)

    dests = (off, right, left, pos)
    sib = [remote(x.at[i], sibin.at[i], s3.at[i], r3.at[i], to_sib) for i in range(4)]

    def for_sib(i):
        down_block(i, dests[i], 1 - co)
        sib[i].start()

    def keep(i):
        down_block(4 + i, dests[i], co)

    def add(slot, half, *refs):
        at = pl.ds(half * HALF, HALF)

        def step(n, carry):
            rows = pl.ds(pl.multiple_of(half * HALF + n * 80, 80), 80)
            local = pl.ds(pl.multiple_of(n * 80, 80), 80)
            total = x[slot, rows].astype(F32)
            for ref in refs:
                total = total + (ref[rows] if ref.shape[0] == ROWS else ref[local]).astype(F32)
            x[slot, rows] = total.astype(BF)
            return carry

        lax.fori_loop(0, HALF // 80, step, 0)

    def ring(n, slot, half, dst, peer):
        return remote(x.at[slot, pl.ds(half * HALF, HALF)], dst, s3.at[n], r3.at[n], peer)

    top, low = pl.ds(0, HALF), pl.ds(HALF, HALF)
    off_r = ring(4, 4, 0, fwd_l, to_r)
    off_l = ring(5, 4, 1, fwd_r, to_l)
    r_low = ring(6, 5, 1, fin_l.at[low], to_r)
    r_top = ring(7, 5, 0, fin_l.at[top], to_r)
    l_top = ring(8, 6, 0, fin_r.at[top], to_l)
    l_low = ring(9, 6, 1, fin_r.at[low], to_l)

    for_sib(0)
    keep(0)
    for_sib(1)
    sib[0].wait_recv()
    add(4, 0, sibin.at[0])
    off_r.start()
    add(4, 1, sibin.at[0])
    off_l.start()
    keep(1)
    for_sib(2)
    sib[1].wait_recv()
    add(5, 1, sibin.at[1])
    r_low.start()
    keep(2)
    sib[2].wait_recv()
    add(6, 0, sibin.at[2])
    l_top.start()
    for_sib(3)
    keep(3)
    off_r.wait_recv()
    add(5, 0, sibin.at[1], fwd_l)
    r_top.start()
    off_l.wait_recv()
    add(6, 1, sibin.at[2], fwd_r)
    l_low.start()
    sib[3].wait_recv()
    for copy in (r_low, l_top, r_top, l_low):
        copy.wait_recv()

    def part(g, carry):
        rows = pl.ds(pl.multiple_of(g * PAIR, PAIR), PAIR)
        total = (x[7, rows].astype(F32) + sibin[3, rows].astype(F32)) + (
            fin_l[rows].astype(F32) + fin_r[rows].astype(F32)
        )
        blank = jnp.zeros((SLAB - USED, QUARTER), F32)
        zout[2 * g] = jnp.concatenate([total[:USED], blank], axis=0).astype(BF)
        zout[2 * g + 1] = jnp.concatenate([total[USED:], blank], axis=0).astype(BF)
        return carry

    lax.fori_loop(0, 8, part, 0)
    moves = []
    for n, ((a, b), peer) in enumerate(zip(ZY, peers)):
        there = ((z + a) % 4) * 4 + (y + b) % 4
        moves.append(remote(zout.at[there], zback.at[here], s4.at[n], r4.at[n], peer))
        moves[-1].start()
    moves.append(pltpu.make_async_copy(zout.at[here], zback.at[here], lsem.at[1]))
    moves[-1].start()
    for copy in sib + [off_r, off_l, r_low, r_top, l_top, l_low]:
        copy.wait_send()
    for copy in moves:
        copy.wait()
    back = zback[...].reshape(EXPERTS * SLAB, QUARTER)
    total = dot(ghi[...], back) + dot(glo[...], back) + state[...].astype(F32)
    mixed[...] = total[:TOK].astype(BF)
    mixed_tan[...] = total[TOK:].astype(BF)


def hbm(n):
    return [pl.BlockSpec(memory_space=pl.ANY)] * n


def vm(n):
    return [pl.BlockSpec(memory_space=VMEM)] * n


def params(cid, mib):
    return pltpu.CompilerParams(collective_id=cid, has_side_effects=True, vmem_limit_bytes=mib * MIB)


def sems(n):
    return pltpu.SemaphoreType.DMA((n,))


def shards(
    residual_in, residual_tan, queries, keys, values, query_tan, key_tan, value_tan,
    out_proj, shift_mod, scale_mod, router, up_weight, down_weight, expert_ids,
):
    shape = jax.ShapeDtypeStruct
    qs, ks = shape((8, TOK, WIDTH), BF), shape((4, TOK, WIDTH), BF)
    qg, qtg, kg, vg, ktg, vtg = pl.pallas_call(
        gather_kernel,
        out_shape=(qs, qs, ks, ks, ks, ks),
        in_specs=hbm(6),
        out_specs=tuple(hbm(6)),
        scratch_shapes=[sems(26), sems(26), sems(6)],
        compiler_params=params(1, 32),
        name="gather_rows",
    )(queries, query_tan, keys, values, key_tan, value_tan)

    two = pl.BlockSpec((2, TOK, WIDTH), lambda i: (i, 0, 0))
    all_keys = pl.BlockSpec((4, TOK, WIDTH), lambda i: (0, 0, 0))
    ot, stats = pl.pallas_call(
        attend_kernel,
        grid=(4,),
        out_shape=(shape((8, TOK, 2 * WIDTH), BF), shape((8, 8, TOK), F32)),
        in_specs=[two, two, all_keys, all_keys, all_keys, all_keys],
        out_specs=(
            pl.BlockSpec((2, TOK, 2 * WIDTH), lambda i: (i, 0, 0)),
            pl.BlockSpec((2, 8, TOK), lambda i: (i, 0, 0)),
        ),
        compiler_params=pltpu.CompilerParams(vmem_limit_bytes=48 * MIB),
        name="attend",
    )(qg, qtg, kg, ktg, vg, vtg)

    spread, info = spread_tables()
    slabs = shape((EXPERTS, SLAB, QUARTER), BF)
    wide = shape((2 * TOK, QUARTER), BF)
    packed, state, ghi, glo = pl.pallas_call(
        middle_kernel,
        out_shape=(slabs, wide, wide, wide),
        in_specs=vm(11),
        out_specs=tuple(vm(4)),
        scratch_shapes=[
            VMEM((8, TOK, 2 * WIDTH), BF),
            VMEM((8, 8, TOK), F32),
            VMEM((2, 2 * TOK, QUARTER), BF),
            VMEM((2, 2 * TOK, QUARTER), BF),
            VMEM((2 * TOK, QUARTER), BF),
            VMEM((2 * TOK, QUARTER), BF),
            VMEM((8, TOK), F32),
            VMEM((3, 8, TOK), F32),
            VMEM((EXPERTS, 2 * TOK), F32),
            VMEM((3, EXPERTS, 2 * TOK), F32),
            VMEM((2 * TOK, WIDTH), BF),
            sems(7), sems(7), sems(7), sems(7), sems(3), sems(3), sems(3), sems(3), sems(3), sems(3), sems(2),
        ],
        compiler_params=params(2, 48),
        name="project_and_pack",
    )(
        ot, stats, out_proj, residual_in, residual_tan,
        shift_mod.reshape(4, QUARTER), scale_mod.reshape(4, QUARTER),
        router.reshape(4, QUARTER, EXPERTS).transpose(0, 2, 1), expert_ids.T,
        jnp.asarray(spread, BF), jnp.asarray(info, F32),
    )

    out = shape((TOK, QUARTER), BF)
    half = VMEM((HALF, QUARTER), BF)
    whole = VMEM((ROWS, QUARTER), BF)
    slab = VMEM((EXPERTS, SLAB, QUARTER), BF)
    return pl.pallas_call(
        expert_kernel,
        out_shape=(out, out),
        in_specs=vm(4) + hbm(2),
        out_specs=tuple(vm(2)),
        scratch_shapes=[
            VMEM((D, HIDDEN), BF),
            VMEM((HIDDEN, D), BF),
            slab,
            VMEM((8, ROWS, QUARTER), BF),
            VMEM((2, ROWS, HIDDEN), F32),
            VMEM((2, ROWS, HIDDEN), BF),
            VMEM((4, ROWS, QUARTER), BF),
            half, half, whole, whole, slab, slab,
            sems(2), sems(15), sems(15), sems(13), sems(13), sems(10), sems(10), sems(15), sems(15), sems(2),
        ],
        compiler_params=params(3, 63),
        name="experts",
    )(packed, state, ghi, glo, up_weight, down_weight)


def solution(mesh):
    rows, heads = P("ctx", "exp"), P("exp", None)
    in_specs = (rows,) * 8 + (
        heads, P(), P(), P(), P("ctx", None, "exp"), P("ctx", "exp", None), P("ctx", None),
    )
    return jax.shard_map(shards, mesh=mesh, in_specs=in_specs, out_specs=(rows, rows), check_vma=False)
```

time: 842 us -> 216 us (0.26); the launches traced: 830 us -> 216 us
  waiting for transfers between devices: 541 us -> 0 us
  Pallas kernels: 0 us -> 203 us
  local copies, waits for them, and re-layouts: 97.7 us -> 12 us
  matrix products: 77.2 us -> 0 us
  starting transfers between devices: 47.7 us -> 0 us
  other arithmetic: 33.8 us -> 0 us
  blocking collectives: 17.8 us -> 0 us
  between operations: 14.9 us -> 0.81 us
    all_gather x4 -> x0, waiting for transfers between devices: 292 us -> none  [the longest x1 79.9 us: shards(): key_piece = lax.all_gather(keys, 'ctx', axis=0, tiled=True)]
    pallas_call x0 -> x4, Pallas kernels: none -> 203 us  [the longest x1 124 us: shards(): pl.pallas_call(expert_kernel, out_shape=(out, out), in_specs=vm(4) + hbm(...]
    all_to_all x4 -> x0, waiting for transfers between devices: 174 us -> none  [the longest x1 58.1 us: shards(): lax.all_to_all(packed, 'ctx', split_axis=0, concat_axis=1, tiled=True)]
    dot_general x15 -> x0, matrix products: 77.2 us -> none  [the longest x1 23 us: shards(): jnp.einsum('rmf,rfd->rmd', act_tan.astype(jnp.bfloat16), down_weight, pre...]
    reduce_scatter x4 -> x0, waiting for transfers between devices: 73.2 us -> none  [the longest x1 24.9 us: shards(): lax.psum_scatter(moe_tan.astype(jnp.bfloat16), 'exp', scatter_dimension=1...]
    all_to_all x4 -> x0, starting transfers between devices: 47.1 us -> none  [the longest x1 15.3 us: shards(): lax.all_to_all(packed_tan, 'ctx', split_axis=0, concat_axis=1, tiled=True)]
    reshape x6 -> x3, local copies, waits for them, and re-layouts: 33.7 us -> 0.03 us  [the longest x1 0.01 us: shards(): shift_mod.reshape(4, QUARTER)]
    reduce_sum x8 -> x0, other arithmetic: 27.3 us -> none  [the longest x1 13.8 us: shards(): jnp.sum(gates_tan[:, :, None] * picked + gates[:, :, None] * picked_tan,...]
  transfers between devices with their start and end apart: 12 -> 0, of which waited for: 12 -> 0; matrix products, arithmetic and copies ran while one was open for 12% -> 0% of each run, Pallas kernels for 0% -> 0%
where the time goes in v1:
time: 216 us
  Pallas kernels  203 us (94%)
  local copies, waits for them, and re-layouts  12 us (6%)
    pallas_call x1, Pallas kernels, shards(): pl.pallas_call(expert_kernel, out_shape=(out, out), in_specs=vm(4) + hbm(...  124 us
    pallas_call x1, Pallas kernels, shards(): pl.pallas_call(middle_kernel, out_shape=(slabs, wide, wide, wide), in_spe...  43.4 us
    pallas_call x1, Pallas kernels, shards(): pl.pallas_call(gather_kernel, out_shape=(qs, qs, ks, ks, ks, ks), in_spec...  27.7 us
    unnamed x38, local copies, waits for them, and re-layouts  11.9 us
    pallas_call x1, Pallas kernels, shards(): pl.pallas_call(attend_kernel, grid=(4,), out_shape=(shape((8, TOK, 2 * WI...  8.01 us

profile of v1, /device:TPU:0, one launch (start us, length us, event | category | flops | bytes accessed | tf_op | source)
XLA Modules:
  0.0 216.0 jit_solution(13722912775512650556)
XLA Ops:
  0.6 0.0 copy-start.4
  0.6 0.0 copy-start.5
  0.7 0.0 copy-start.6
  0.7 0.9 copy-done.6
  1.6 0.9 copy-done.7
  2.5 0.9 copy-done.8
  3.4 0.9 copy-done.9
  4.3 0.9 copy-done.10
  5.2 0.9 copy-done.11
  6.1 0.0 copy-start.13
  6.1 0.0 copy-start.14
  6.1 27.7 %gather_rows.1 = (bf16[8,128,384]{2,1,0:T(8,128)(2,1)S(1)}, bf16[8,128,384]{2,1,0:T(8,128)(2,1)S(1)}, bf16[4,128,384]{2,1,0:T(8,128)(2,1)S(1)}, bf16[4,128,384]{...) custom-call(bf16[128,384]{1,0:T(8,128)(2,1)S(1)} %copy-done.6, ...), custom_call_target="tpu_custom_call" | custom-call | tf_op jit(solution)/shard_map/gather_rows/pallas_call | solution.py:549
  33.8 8.0 %attend.1 = (bf16[8,128,768]{2,1,0:T(8,128)(2,1)S(1)}, f32[8,8,128]{2,1,0:T(8,128)S(1)}) custom-call(bf16[8,128,384]{2,1,0:T(8,128)(2,1)S(1)} %get-tuple-element.14.q, bf16[8,128,384]{2,1,0:T(8,128)(2,1)S(1)} %get-tuple-element.15.qt, bf16[4,128,384]{2,1,0:T(8,128)(2,1)S(1)} %get-tuple-element.16.k, bf16[4,128,384]{2,1,0:T(8,128)(2,1)S(1)} %get-tuple-element.17.kt, ...), custom_call_target="tpu_custom_call" | custom-call | tf_op jit(solution)/shard_map/attend/pallas_call | solution.py:561
  41.8 0.0 copy-done.15
  41.9 0.0 copy-done.16
  42.0 43.4 %project_and_pack.1 = (bf16[16,48,768]{2,1,0:T(8,128)(2,1)S(1)}, bf16[256,768]{1,0:T(8,128)(2,1)S(1)}, bf16[256,768]{1,0:T(8,128)(2,1)S(1)}, bf16[256,768]{1,0:T(8,128)(2,1)S(1)}) custom-call(bf16[8,128,768]{2,1,0:T(8,128)(2,1)S(1)} %get-tuple-element.20.ot, f32[8,8,128]{2,1,0:T(8,128)S(1)} %get-tuple-element.21.stats, bf16[384,3072]{1,0:T(8,128)(2,1)} %out_proj.1, ...), custom_call_target="tpu_custom_call" | custom-call | tf_op jit(solution)/shard_map/project_and_pack/pallas_call | solution.py:577
  85.4 0.0 copy-start
  85.4 1.0 copy-done
  86.4 0.7 copy-done.1
  87.2 0.8 copy-done.2
  87.9 0.7 copy-done.3
  88.7 124.0 %experts.1 = (bf16[128,768]{1,0:T(8,128)(2,1)}, bf16[128,768]{1,0:T(8,128)(2,1)}) custom-call(bf16[16,48,768]{2,1,0:T(8,128)(2,1)} %copy-done, bf16[256,768]{1,0:T(8,128)(2,1)} %copy-done.1, bf16[256,768]{1,0:T(8,128)(2,1)} %copy-done.2, bf16[256,768]{1,0:T(8,128)(2,1)} %copy-done.3, bf16[1,3072,1536]{2,1,0:T(8,128)(2,1)} %up.1, bf16[1,1536,3072]{2,1,0:T(8,128)(2,1)} %down.1), custom_call_target="tpu_custom_call" | custom-call | tf_op jit(solution)/shard_map/experts/pallas_call | solution.py:609
  212.7 1.6 copy.25
  214.4 1.6 copy.26
  (21 shorter events, 0.1 us)
Async XLA Ops:
  0.6 41.3 %copy-start.4 = (bf16[128,768]{1,0:T(8,128)(2,1)S(1)}, bf16[128,768]{1,0:T(8,128)(2,1)}, u32[]{:S(2)}) copy-start(bf16[128,768]{1,0:T(8,128)(2,1)} %res.1) | copy-start | bytes 589828
  0.6 41.3 %copy-start.5 = (bf16[128,768]{1,0:T(8,128)(2,1)S(1)}, bf16[128,768]{1,0:T(8,128)(2,1)}, u32[]{:S(2)}) copy-start(bf16[128,768]{1,0:T(8,128)(2,1)} %rest.1) | copy-start | bytes 589828
  0.7 0.9 copy-start.6
  1.6 0.9 copy-start.7
  2.5 0.9 copy-start.8
  3.4 0.9 copy-start.9
  4.3 0.9 copy-start.10
  5.2 0.9 copy-start.11
  6.1 35.8 %copy-start.15 = (bf16[3072,16]{0,1:T(8,128)(2,1)S(1)}, bf16[3072,16]{0,1:T(8,128)(2,1)}, u32[]{:S(2)}) copy-start(bf16[3072,16]{0,1:T(8,128)(2,1)} %param.28) | copy-start | bytes 294916
  6.1 35.8 %copy-start.16 = (f32[3072]{0:T(1024)S(1)}, f32[3072]{0:T(1024)}, u32[]{:S(2)}) copy-start(f32[3072]{0:T(1024)} %param.26) | copy-start | bytes 36868
  6.1 35.8 %copy-start.17 = (f32[3072]{0:T(1024)S(1)}, f32[3072]{0:T(1024)}, u32[]{:S(2)}) copy-start(f32[3072]{0:T(1024)} %param.27) | copy-start | bytes 36868
  6.1 35.9 %copy-start.12 = (bf16[16,768]{1,0:T(8,128)(2,1)S(1)}, bf16[16,768]{1,0:T(8,128)(2,1)}, u32[]{:S(2)}) copy-start(bf16[16,768]{1,0:T(8,128)(2,1)} %constant.4.clone.spread) | copy-start | bytes 73732
  6.1 35.9 %copy-start.13 = (f32[8,768]{1,0:T(8,128)S(1)}, f32[8,768]{1,0:T(8,128)}, u32[]{:S(2)}) copy-start(f32[8,768]{1,0:T(8,128)} %constant.5.clone.info) | copy-start | bytes 73732
  6.1 35.9 %copy-start.14 = (s32[128,2]{0,1:T(2,128)S(1)}, s32[128,2]{0,1:T(2,128)}, u32[]{:S(2)}) copy-start(s32[128,2]{0,1:T(2,128)} %param.31) | copy-start | bytes 3076
  85.4 1.0 copy-start
  86.4 0.7 copy-start.1
  87.2 0.8 copy-start.2
  87.9 0.7 copy-start.3

commit v2 on v0

v2 whole, which is shorter than its diff:
```python
import functools
import types

import jax
import jax.numpy as jnp
from jax import lax
from jax.experimental import pallas as pl
from jax.experimental.pallas import tpu as pltpu
from jax.sharding import PartitionSpec as P

D = 3072
HD = 128
TOK = 128
HEADS_HERE = 3
WIDTH = HEADS_HERE * HD
QUARTER = 768
EXPERTS = 16
CAP = 20
MAIN = 16
GROUP = 4 * CAP
ROWS = 640
HALF = ROWS // 2
COLS = QUARTER // 2
HIDDEN = 1536
EPS = 1e-06
FACTOR = HD ** (-0.5)
LOG2E = 1.4426950408889634
MIB = 2**20

BF = jnp.bfloat16
F32 = jnp.float32
MESH = pl.DeviceIdType.MESH
VMEM = pltpu.VMEM
NT = (((1,), (1,)), ((), ()))
TN = (((0,), (0,)), ((), ()))
NN = (((1,), (0,)), ((), ()))


def dot(a, b, dims=NN):
    return lax.dot_general(a, b, dims, preferred_element_type=F32)


def coords():
    c = lax.axis_index("ctx")
    e = lax.axis_index("exp")
    return c // 8, (c // 2) % 4, c % 2, e // 2, e % 2


def device(z, y, xh, xl, core):
    return (z * 8 + y * 2 + xh, xl * 2 + core)


def meet(peers):
    barrier = pltpu.get_barrier_semaphore()
    for peer in peers:
        pl.semaphore_signal(barrier, inc=1, device_id=peer, device_id_type=MESH)
    pl.semaphore_wait(barrier, len(peers))


def remote(src, dst, send, recv, peer):
    return pltpu.make_async_remote_copy(
        src_ref=src, dst_ref=dst, send_sem=send, recv_sem=recv, device_id=peer, device_id_type=MESH
    )


YX = [(0, 1)] + [(a, b) for a in (1, 3, 2) for b in (0, 1)]
ZY = [(a, b) for a in (2, 1, 3, 0) for b in (2, 1, 3, 0) if a or b]

INPUTS = (
    "q", "qt", "k", "v", "kt", "vt", "out_proj", "res", "rest", "up", "down", "router",
    "shift", "scale", "ids",
)
OUTPUTS = ("mixed", "mixed_tan")


def sems(n):
    return pltpu.SemaphoreType.DMA((n,))


SCRATCH = {
    "qg": VMEM((8, TOK, WIDTH), BF),
    "qtg": VMEM((8, TOK, WIDTH), BF),
    "kg": VMEM((4, TOK, WIDTH), BF),
    "ktg": VMEM((4, TOK, WIDTH), BF),
    "vg": VMEM((4, TOK, WIDTH), BF),
    "vtg": VMEM((4, TOK, WIDTH), BF),
    "ot": VMEM((2, 8, TOK, WIDTH), BF),
    "got": VMEM((2, 8, TOK, WIDTH), BF),
    "stats": VMEM((8, 8, TOK), F32),
    "gstats": VMEM((8, 8, TOK), F32),
    "proj": VMEM((WIDTH, D), BF),
    "state": VMEM((2, TOK, QUARTER), BF),
    "routerv": VMEM((EXPERTS, QUARTER), BF),
    "shiftv": VMEM((1, QUARTER), F32),
    "scalev": VMEM((1, QUARTER), F32),
    "idsv": VMEM((2, TOK), jnp.int32),
    "mine": VMEM((2, 2, TOK, QUARTER), BF),
    "sib": VMEM((2, 2, TOK, QUARTER), BF),
    "far": VMEM((2, TOK, QUARTER), BF),
    "farin": VMEM((2, TOK, QUARTER), BF),
    "mstat": VMEM((2, 8, TOK), F32),
    "gstat": VMEM((2, 3, 8, TOK), F32),
    "mlog": VMEM((EXPERTS, 2 * TOK), F32),
    "glog": VMEM((3, EXPERTS, 2 * TOK), F32),
    "acc": VMEM((2, TOK, WIDTH), BF),
    "kept": VMEM((TOK, QUARTER), F32),
    "normed": VMEM((2, TOK, QUARTER), BF),
    "gates": VMEM((4, 2 * TOK, 256), BF),
    "pmain": VMEM((2, EXPERTS, MAIN, QUARTER), BF),
    "prest": VMEM((2, EXPERTS, MAIN, 256), BF),
    "zrest": VMEM((2, EXPERTS, MAIN, 256), BF),
    "upv": VMEM((D, HIDDEN), BF),
    "downv": VMEM((HIDDEN, D), BF),
    "x": VMEM((8, ROWS, QUARTER), BF),
    "pre": VMEM((HALF, HIDDEN), F32),
    "slope": VMEM((2, HALF, HIDDEN), BF),
    "act": VMEM((2, 2, HALF, HIDDEN), BF),
    "down_out": VMEM((8, HALF, QUARTER), BF),
    "sibin": VMEM((2, 4, HALF, QUARTER), BF),
    "fwd_l": VMEM((2, HALF, COLS), BF),
    "fwd_r": VMEM((2, HALF, COLS), BF),
    "fin_l": VMEM((2, HALF, QUARTER), BF),
    "fin_r": VMEM((2, HALF, QUARTER), BF),
    "total": VMEM((2, HALF, QUARTER), BF),
    "trest": VMEM((2, EXPERTS, MAIN, 256), BF),
    "bmain": VMEM((2, EXPERTS, MAIN, QUARTER), BF),
    "brest": VMEM((2, EXPERTS, MAIN, 256), BF),
    "lsem": sems(27),
    "kv_s": sems(12), "kv_r": sems(12),
    "q_s": sems(16), "q_r": sems(16),
    "o_s": sems(24), "o_r": sems(24),
    "p_s": sems(6), "p_r": sems(6),
    "t_s": sems(6), "t_r": sems(6),
    "g_s": sems(3), "g_r": sems(3),
    "z_s": sems(60), "z_r": sems(60),
    "a_s": sems(22), "a_r": sems(22),
    "r_s": sems(20), "r_r": sems(20),
    "b_s": sems(60), "b_r": sems(60),
}


def to_columns(rows):
    n = rows.shape[0]
    return jnp.concatenate([rows, jnp.zeros((128 - n, 128), F32)], axis=0).T


def attend(r, yp):
    at = pl.ds(2 * yp, 2)
    for h in range(HEADS_HERE):
        c = slice(h * HD, (h + 1) * HD)
        qh, qth = r.qg[at, :, c].reshape(256, HD), r.qtg[at, :, c].reshape(256, HD)
        kh, kth = r.kg[:, :, c].reshape(512, HD), r.ktg[:, :, c].reshape(512, HD)
        vh, vth = r.vg[:, :, c].reshape(512, HD), r.vtg[:, :, c].reshape(512, HD)
        scores = dot(kh, qh, NT) * (FACTOR * LOG2E)
        tan = dot(jnp.concatenate([kh, kth], 1), jnp.concatenate([qth, qh], 1), NT) * FACTOR
        high = jnp.max(scores, axis=0, keepdims=True)
        weights = jnp.exp2(scores - high)
        total = jnp.sum(weights, axis=0, keepdims=True)
        weights = weights * (1.0 / total)
        mean = jnp.sum(weights * tan, axis=0, keepdims=True)
        tilted = (weights * (tan - mean)).astype(BF)
        both = dot(weights.astype(BF), jnp.concatenate([vh, vth], 1), TN)
        tout = both[:, HD:] + dot(tilted, vh, TN)
        r.ot[0, at, :, c] = both[:, :HD].astype(BF).reshape(2, TOK, HD)
        r.ot[1, at, :, c] = tout.astype(BF).reshape(2, TOK, HD)
        lse = high + jnp.log2(total)
        for i in range(2):
            part = slice(i * TOK, (i + 1) * TOK)
            r.stats[2 * yp + i, h : h + 1, :] = lse[:, part]
            r.stats[2 * yp + i, 4 + h : 5 + h, :] = mean[:, part]


def curves(x):
    sq = x * x
    th = jnp.tanh(0.7978845608028654 * x * (1.0 + 0.044715 * sq))
    half = 0.5 * (1.0 + th)
    slope = half + 0.5 * x * (1.0 - th * th) * (0.7978845608028654 * (1.0 + 0.134145 * sq))
    return x * half, slope


def block_kernel(*refs):
    r = types.SimpleNamespace(**dict(zip(INPUTS + OUTPUTS + tuple(SCRATCH), refs)))
    z, y, xh, xl, co = coords()
    e = xl * 2 + co
    pos = xh * 2 + xl
    here_q = y * 2 + xh
    here = z * 4 + y
    right, left, off = (pos + 1) % 4, (pos + 3) % 4, (pos + 2) % 4
    pair, other = xh * 2 + 1 - xl, (1 - xh) * 2 + 1 - xl

    def at_pos(p, c):
        return device(z, y, p // 2, p % 2, c)

    def near(a, b):
        return device(z, (y + a) % 4, (xh + b) % 2, xl, co)

    to_r, to_l, to_sib = at_pos(right, co), at_pos(left, co), at_pos(pos, 1 - co)
    across, diagonal = at_pos(pair, co), at_pos(pair, 1 - co)
    peers_e = [to_sib, across, diagonal]
    peers_zy = [device((z + a) % 4, (y + b) % 4, xh, xl, co) for a, b in ZY]
    meet(peers_zy + [near(a, 1) for a in range(4)] + peers_e + [at_pos(other, co)])

    kv = []
    for n, a in enumerate((1, 3, 2)):
        peer = device((z + a) % 4, y, xh, xl, co)
        for i, (src, dst) in enumerate(((r.k, r.kg), (r.kt, r.ktg), (r.v, r.vg), (r.vt, r.vtg))):
            kv.append(remote(src, dst.at[z], r.kv_s.at[n * 4 + i], r.kv_r.at[n * 4 + i], peer))
            kv[-1].start()

    def q_copies(a, b):
        n = 4 * a + 2 * b
        return [
            remote(src, dst.at[here_q], r.q_s.at[n + i], r.q_r.at[n + i], near(a, b))
            for i, (src, dst) in enumerate(((r.q, r.qg), (r.qt, r.qtg)))
        ]

    for a, b in YX:
        for copy in q_copies(a, b):
            copy.start()
    quarter = pl.ds(pl.multiple_of(e * QUARTER, QUARTER), QUARTER)
    local = [
        pltpu.make_async_copy(src, dst, r.lsem.at[i])
        for i, (src, dst) in enumerate(
            (
                (r.k, r.kg.at[z]), (r.kt, r.ktg.at[z]), (r.v, r.vg.at[z]), (r.vt, r.vtg.at[z]),
                (r.q, r.qg.at[here_q]), (r.qt, r.qtg.at[here_q]),
                (r.out_proj, r.proj), (r.res, r.state.at[0]), (r.rest, r.state.at[1]),
                (r.router.at[:, quarter], r.routerv),
                (r.shift.at[:, quarter], r.shiftv), (r.scale.at[:, quarter], r.scalev), (r.ids, r.idsv),
                (r.up.at[0], r.upv), (r.down.at[0], r.downv),
            )
        )
    ]
    for copy in local:
        copy.start()

    r.stats[...] = jnp.zeros_like(r.stats)
    local[12].wait()
    expert = lax.broadcasted_iota(jnp.int32, (EXPERTS, TOK), 0)
    oh0 = (r.idsv[0:1, :] == expert).astype(F32)
    oh1 = (r.idsv[1:2, :] == expert).astype(F32)
    named = (oh0 + oh1).astype(BF)

    def iota(shape, dim):
        return lax.broadcasted_iota(jnp.int32, shape, dim)

    before = (iota((TOK, TOK), 0) < iota((TOK, TOK), 1)).astype(BF)
    rank = dot(named, before).astype(BF)
    spread = (iota((EXPERTS, 256), 1) // MAIN == iota((EXPERTS, 256), 0)).astype(BF)

    def selection():
        named_x = dot(named, spread, TN)
        rank_x = dot(rank, spread, TN)
        slot = iota((TOK, 256), 1) % MAIN
        main = jnp.where(rank_x == slot.astype(F32), named_x, 0.0)
        rest = jnp.where(rank_x == (MAIN + slot % 4).astype(F32), named_x, 0.0)
        return main, rest, slot // 4

    def out_copies(a, b, part):
        n = 6 * a + 3 * b
        there = ((y + a) % 4) * 2 + (xh + b) % 2
        moves = [
            remote(
                r.ot.at[part, there], r.got.at[part, here_q], r.o_s.at[n + part], r.o_r.at[n + part], near(a, b)
            )
        ]
        if part == 0:
            moves.append(
                remote(r.stats.at[there], r.gstats.at[here_q], r.o_s.at[n + 2], r.o_r.at[n + 2], near(a, b))
            )
        return moves

    for copy in local[:6]:
        copy.wait()
    for copy in kv:
        copy.wait_recv()
    for copy in q_copies(0, 1):
        copy.wait_recv()
    attend(r, y)
    for copy in out_copies(0, 1, 0):
        copy.start()
    keep = [
        pltpu.make_async_copy(r.stats.at[here_q], r.gstats.at[here_q], r.lsem.at[23]),
        pltpu.make_async_copy(r.ot.at[0, here_q], r.got.at[0, here_q], r.lsem.at[24]),
        pltpu.make_async_copy(r.ot.at[1, here_q], r.got.at[1, here_q], r.lsem.at[25]),
    ]
    for copy in keep:
        copy.start()

    def attend_step(i, carry):
        a = 1 + 2 * i - 3 * (i // 2)
        for b in (0, 1):
            for copy in q_copies(a, b):
                copy.wait_recv()
        attend(r, (y + 4 - a) % 4)
        for b in (0, 1):
            for copy in out_copies(4 - a, b, 0):
                copy.start()
        return carry

    lax.fori_loop(0, 3, attend_step, 0)
    for a, b in YX:
        out_copies(a, b, 1)[0].start()
    for copy in kv:
        copy.wait_send()
    for a, b in YX:
        for copy in q_copies(a, b):
            copy.wait_send()
    for copy in local[6:12] + keep:
        copy.wait()
    for a, b in YX:
        for copy in out_copies(a, b, 0):
            copy.wait()

    lse = [r.gstats[j, 0:3, :] for j in range(8)]
    mean = [r.gstats[j, 4:7, :] for j in range(8)]
    top = functools.reduce(jnp.maximum, lse)
    part = [jnp.exp2(item - top) for item in lse]
    inv = 1.0 / functools.reduce(jnp.add, part)
    part = [item * inv for item in part]
    mid = functools.reduce(jnp.add, [p * m for p, m in zip(part, mean)])
    lean = [p * (m - mid) for p, m in zip(part, mean)]
    cols = to_columns(jnp.concatenate(part + lean, axis=0))

    def merge(pt):
        for h in range(HEADS_HERE):
            at = slice(h * HD, (h + 1) * HD)
            sum_ = jnp.zeros((TOK, HD), F32)
            for j in range(8):
                w = cols[:, j * 3 + h : j * 3 + h + 1]
                sum_ = sum_ + w * r.got[pt, j, :, at].astype(F32)
                if pt == 1:
                    c = cols[:, 24 + j * 3 + h : 24 + j * 3 + h + 1]
                    sum_ = sum_ + c * r.got[0, j, :, at].astype(F32)
            r.acc[pt, :, at] = sum_.astype(BF)

    def project(pt, xl_to, core_to):
        at = pl.multiple_of((xl_to * 2 + core_to) * QUARTER, QUARTER)
        return dot(r.acc[pt], r.proj[:, pl.ds(at, QUARTER)])

    def project_move(pt, n, src, dst, peer):
        return remote(src, dst, r.p_s.at[pt * 3 + n], r.p_r.at[pt * 3 + n], peer)

    to_sib0 = [project_move(pt, 0, r.mine.at[pt, 0], r.sib.at[pt, 0], to_sib) for pt in range(2)]
    to_sib1 = [project_move(pt, 1, r.mine.at[pt, 1], r.sib.at[pt, 1], to_sib) for pt in range(2)]
    to_far = [project_move(pt, 2, r.far.at[pt], r.farin.at[pt], across) for pt in range(2)]

    def start_projection(pt):
        r.mine[pt, 0] = project(pt, 1 - xl, 1 - co).astype(BF)
        to_sib0[pt].start()
        r.mine[pt, 1] = project(pt, xl, 1 - co).astype(BF)
        to_sib1[pt].start()
        away = project(pt, 1 - xl, co)
        to_sib0[pt].wait()
        r.far[pt] = (away + r.sib[pt, 0].astype(F32)).astype(BF)
        to_far[pt].start()
        kept = project(pt, xl, co)
        to_sib1[pt].wait()
        r.kept[...] = kept + r.sib[pt, 1].astype(F32) + r.state[pt].astype(F32)

    def end_projection(pt):
        to_far[pt].wait()
        r.state[pt] = (r.kept[...] + r.farin[pt].astype(F32)).astype(BF)

    def start_mean(pt):
        product = jnp.sum(r.state[0].astype(F32) * r.state[pt].astype(F32), axis=1, keepdims=True)
        r.mstat[pt] = jnp.broadcast_to(product, (TOK, 128)).T[0:8]
        moves = [
            remote(r.mstat.at[pt], r.gstat.at[pt, n], r.t_s.at[pt * 3 + n], r.t_r.at[pt * 3 + n], peer)
            for n, peer in enumerate(peers_e)
        ]
        for copy in moves:
            copy.start()
        return moves

    def end_mean(pt, moves):
        for copy in moves:
            copy.wait()
        rows = (r.mstat[pt] + r.gstat[pt, 0]) + (r.gstat[pt, 1] + r.gstat[pt, 2])
        return to_columns(rows)[:, 0:1] * (1.0 / D)

    block = pos * 2 + co

    def rows_of(source):
        return pl.ds(pl.multiple_of((source // 4) * GROUP + (source % 4) * MAIN, MAIN), MAIN)

    def x_rows_of(pt, source):
        return pl.ds(pl.multiple_of(pt * HALF + (source // 4) * GROUP + (source % 4) * MAIN, MAIN), MAIN)

    def plane(pt, main, rest, send, recv, lsem):
        moves = []
        for i, (src, dst) in enumerate((main, rest)):
            for n, ((a, b), peer) in enumerate(zip(ZY, peers_zy)):
                there = ((z + a) % 4) * 4 + (y + b) % 4
                at = pt * 30 + i * 15 + n
                moves.append(remote(src(there), dst(here), send.at[at], recv.at[at], peer))
            moves.append(pltpu.make_async_copy(src(here), dst(here), r.lsem.at[lsem + 2 * pt + i]))
        for copy in moves:
            copy.start()
        return moves

    def route(pt):
        main, rest, piece = selection()
        rows = r.normed[pt]
        r.pmain[pt] = dot(main.astype(BF), rows, TN).astype(BF).reshape(EXPERTS, MAIN, QUARTER)
        value = jnp.zeros((256, 256), F32)
        for g in range(3):
            chosen = jnp.where(piece == g, rest, 0.0).astype(BF)
            value = value + dot(chosen, rows[:, g * 256 : (g + 1) * 256], TN)
        r.prest[pt] = value.astype(BF).reshape(EXPERTS, MAIN, 256)
        return plane(
            pt,
            (lambda s: r.pmain.at[pt, s], lambda s: r.x.at[block, x_rows_of(pt, s)]),
            (lambda s: r.prest.at[pt, s], lambda s: r.zrest.at[pt, s]),
            r.z_s, r.z_r, 15,
        )

    def piece_rows(g):
        to, source = iota((64, 256), 0), iota((64, 256), 1)
        return ((to // 4 == source // MAIN) & (source % MAIN == 4 * g + to % 4)).astype(BF)

    def end_route(pt, moves):
        for copy in moves:
            copy.wait()
        rest = r.zrest[pt].reshape(256, 256)
        for g in range(3):
            value = dot(piece_rows(g), rest).astype(BF)
            for i in range(4):
                at = slice(pt * HALF + i * GROUP + 64, pt * HALF + (i + 1) * GROUP)
                r.x[block, at, g * 256 : (g + 1) * 256] = value[i * 16 : (i + 1) * 16]

    x = r.x
    bl, br, bo = left * 2 + co, right * 2 + co, off * 2 + co

    def half_cols(h):
        return pl.ds(h * COLS, COLS)

    def pass_on(pt, n, b, h, peer):
        cols = pl.ds(0, QUARTER) if h is None else half_cols(h)
        ref = x.at[b, pl.ds(pt * HALF, HALF), cols]
        return remote(ref, ref, r.a_s.at[pt * 11 + n], r.a_r.at[pt * 11 + n], peer)

    def ring_copies(pt):
        return types.SimpleNamespace(
            own=pass_on(pt, 0, block, None, to_sib),
            r0=pass_on(pt, 1, block, 0, to_r),
            r1=pass_on(pt, 2, block, 1, to_r),
            l1=pass_on(pt, 3, block, 1, to_l),
            l0=pass_on(pt, 4, block, 0, to_l),
            fr=pass_on(pt, 5, bl, 0, to_r),
            fl=pass_on(pt, 6, br, 1, to_l),
            sl=pass_on(pt, 7, bl, None, to_sib),
            sr=pass_on(pt, 8, br, None, to_sib),
            s0=pass_on(pt, 9, bo, 0, to_sib),
            s1=pass_on(pt, 10, bo, 1, to_sib),
        )

    spin = [ring_copies(pt) for pt in range(2)]

    def start_ring(pt):
        c = spin[pt]
        for copy in (c.r0, c.l1, c.r1, c.l0, c.own):
            copy.start()

    def forward_far(pt):
        c = spin[pt]
        c.r0.wait_recv()
        c.fr.start()
        c.l1.wait_recv()
        c.fl.start()

    def forward_near(pt):
        c = spin[pt]
        c.r1.wait_recv()
        c.sl.start()
        c.l0.wait_recv()
        c.sr.start()

    def end_ring(pt):
        c = spin[pt]
        c.fr.wait_recv()
        c.s0.start()
        c.fl.wait_recv()
        c.s1.start()

    def up_tile(pt, p, n):
        cols = pl.ds(pl.multiple_of(n * 512, 512), 512)
        a = pl.ds(pl.multiple_of((p % 2) * HIDDEN, HIDDEN), QUARTER)
        b = pl.ds(pl.multiple_of((p % 2) * HIDDEN + QUARTER, QUARTER), QUARTER)
        rows = slice(pt * HALF, (pt + 1) * HALF)
        return dot(x[2 * p, rows], r.upv[a, cols]) + dot(x[2 * p + 1, rows], r.upv[b, cols]), cols

    def up_first(pt, p):
        def tile(n, carry):
            value, cols = up_tile(pt, p, n)
            r.pre[:, cols] = value
            return carry

        lax.fori_loop(0, 3, tile, 0)

    def up_second(pt, p, at):
        def tile(n, carry):
            value, cols = up_tile(pt, p, n)
            value = r.pre[:, cols] + value
            if pt == 0:
                value, slope = curves(value)
                r.slope[at, :, cols] = slope.astype(BF)
            else:
                value = value * r.slope[at, :, cols].astype(F32)
            r.act[pt, at, :, cols] = value.astype(BF)
            return carry

        lax.fori_loop(0, 3, tile, 0)

    dests = (off, right, left, pos)

    def out_ref(pt, i):
        return r.down_out.at[i] if pt == 0 else x.at[i, pl.ds(0, HALF)]

    def down_part(pt, i, core_to):
        p = dests[i]
        at = jnp.where(p // 2 == xh, 0, 1)
        cols = pl.ds(pl.multiple_of(((p % 2) * 2 + core_to) * QUARTER, QUARTER), QUARTER)
        out_ref(pt, 2 * i + (0 if core_to is not co else 1))[...] = dot(r.act[pt, at], r.downv[:, cols]).astype(BF)

    def add(pt, i, h, *more):
        dst = out_ref(pt, 2 * i + 1)
        cols = slice(h * COLS, (h + 1) * COLS)

        def step(n, carry):
            at = pl.ds(pl.multiple_of(n * 80, 80), 80)
            value = dst[at, cols].astype(F32) + r.sibin[pt, i, at, cols].astype(F32)
            for ref in more:
                value = value + ref[pt, at].astype(F32)
            dst[at, cols] = value.astype(BF)
            return carry

        lax.fori_loop(0, HALF // 80, step, 0)

    def sum_copies(pt):
        def move(n, src, dst, peer):
            return remote(src, dst, r.r_s.at[pt * 10 + n], r.r_r.at[pt * 10 + n], peer)

        def piece(i, h):
            return out_ref(pt, 2 * i + 1).at[:, half_cols(h)]

        return types.SimpleNamespace(
            sib=[move(i, out_ref(pt, 2 * i), r.sibin.at[pt, i], to_sib) for i in range(4)],
            off_r=move(4, piece(0, 0), r.fwd_l.at[pt], to_r),
            off_l=move(5, piece(0, 1), r.fwd_r.at[pt], to_l),
            r0=move(6, piece(1, 0), r.fin_l.at[pt, :, half_cols(0)], to_r),
            r1=move(7, piece(1, 1), r.fin_l.at[pt, :, half_cols(1)], to_r),
            l0=move(8, piece(2, 0), r.fin_r.at[pt, :, half_cols(0)], to_l),
            l1=move(9, piece(2, 1), r.fin_r.at[pt, :, half_cols(1)], to_l),
        )

    sums = [sum_copies(pt) for pt in range(2)]

    def both_parts(pt, i):
        down_part(pt, i, 1 - co)
        sums[pt].sib[i].start()
        down_part(pt, i, co)

    def start_sums(pt):
        c = sums[pt]
        c.sib[0].wait_recv()
        add(pt, 0, 0)
        c.off_r.start()
        add(pt, 0, 1)
        c.off_l.start()

    def neighbour_sums(pt):
        c = sums[pt]
        c.sib[1].wait_recv()
        add(pt, 1, 1)
        c.r1.start()
        c.sib[2].wait_recv()
        add(pt, 2, 0)
        c.l0.start()

    def forward_sums(pt):
        c = sums[pt]
        c.off_r.wait_recv()
        add(pt, 1, 0, r.fwd_l)
        c.r0.start()
        c.off_l.wait_recv()
        add(pt, 2, 1, r.fwd_r)
        c.l1.start()

    def leave(pt):
        c = sums[pt]
        for copy in (c.sib[3], c.r1, c.l0, c.r0, c.l1):
            copy.wait_recv()
        own = out_ref(pt, 7)

        def step(g, carry):
            at = pl.ds(pl.multiple_of(g * GROUP, GROUP), GROUP)
            value = (own[at].astype(F32) + r.sibin[pt, 3, at].astype(F32)) + (
                r.fin_l[pt, at].astype(F32) + r.fin_r[pt, at].astype(F32)
            )
            r.total[pt, at] = value.astype(BF)
            return carry

        lax.fori_loop(0, 4, step, 0)
        rest = jnp.concatenate([r.total[pt, i * GROUP + 64 : (i + 1) * GROUP] for i in range(4)], axis=0)
        value = jnp.zeros((256, 256), F32)
        for g in range(3):
            value = value + dot(piece_rows(g), rest[:, g * 256 : (g + 1) * 256], TN)
        r.trest[pt] = value.astype(BF).reshape(EXPERTS, MAIN, 256)
        return plane(
            pt,
            (lambda s: r.total.at[pt, rows_of(s)], lambda s: r.bmain.at[pt, s]),
            (lambda s: r.trest.at[pt, s], lambda s: r.brest.at[pt, s]),
            r.b_s, r.b_r, 19,
        )

    merge(0)
    start_projection(0)
    end_projection(0)
    moves = start_mean(0)
    gain = 1.0 + r.scalev[...]
    recip = lax.rsqrt(end_mean(0, moves) + EPS)
    sf = r.state[0].astype(F32)
    r.normed[0] = (sf * recip * gain + r.shiftv[...]).astype(BF)
    route0 = route(0)

    for a, b in YX:
        out_copies(a, b, 1)[0].wait()
    merge(1)
    start_projection(1)
    end_route(0, route0)
    start_ring(0)
    end_projection(1)
    moves = start_mean(1)
    cross = end_mean(1, moves)
    sf, tf = r.state[0].astype(F32), r.state[1].astype(F32)
    r.normed[1] = ((tf * recip - sf * (recip * recip * recip) * cross) * gain).astype(BF)
    route1 = route(1)
    both = r.normed[...].reshape(2 * TOK, QUARTER)
    r.mlog[...] = dot(r.routerv[...], both, NT)
    log_moves = [
        remote(r.mlog, r.glog.at[n], r.g_s.at[n], r.g_r.at[n], peer) for n, peer in enumerate(peers_e)
    ]
    for copy in log_moves:
        copy.start()

    for copy in local[13:]:
        copy.wait()
    c0, c1 = spin
    c0.own.wait_recv()
    up_first(0, pos)
    forward_far(0)
    forward_near(0)
    end_route(1, route1)
    start_ring(1)
    c0.sl.wait_recv()
    c0.sr.wait_recv()
    up_second(0, pair, 0)
    end_ring(0)
    up_first(0, other)
    c0.s0.wait_recv()
    c0.s1.wait_recv()
    up_second(0, off, 1)
    both_parts(0, 0)
    forward_far(1)
    start_sums(0)
    forward_near(1)
    c1.own.wait_recv()
    up_first(1, pos)
    both_parts(0, 1)
    c1.sl.wait_recv()
    c1.sr.wait_recv()
    up_second(1, pair, 0)
    end_ring(1)
    both_parts(0, 2)
    neighbour_sums(0)
    forward_sums(0)
    up_first(1, other)
    c1.s0.wait_recv()
    c1.s1.wait_recv()
    up_second(1, off, 1)
    for c in spin:
        for copy in vars(c).values():
            copy.wait_send()
    both_parts(1, 0)
    both_parts(0, 3)
    start_sums(1)
    both_parts(1, 1)
    both_parts(1, 2)
    neighbour_sums(1)
    back0 = leave(0)
    forward_sums(1)
    both_parts(1, 3)

    for copy in log_moves:
        copy.wait()
    logits = (r.mlog[...] + r.glog[0]) + (r.glog[1] + r.glog[2])
    ll, lt = logits[:, :TOK], logits[:, TOK:]
    own0 = jnp.sum(oh0 * ll, axis=0, keepdims=True)
    own1 = jnp.sum(oh1 * ll, axis=0, keepdims=True)
    diff = jnp.sum(oh0 * lt, axis=0, keepdims=True) - jnp.sum(oh1 * lt, axis=0, keepdims=True)
    gate0 = 1.0 / (1.0 + jnp.exp(own1 - own0))
    gate1 = 1.0 / (1.0 + jnp.exp(own0 - own1))
    gates = oh0 * gate0 + oh1 * gate1
    gates_tan = oh0 * (gate0 * (1.0 - gate0) * diff) - oh1 * (gate1 * (1.0 - gate1) * diff)
    main, rest, piece = selection()
    for i, g in enumerate((gates, gates_tan)):
        high = g.astype(BF)
        low = (g - high.astype(F32)).astype(BF)
        at = slice(i * TOK, (i + 1) * TOK)
        for j, item in enumerate((high, low)):
            wide = dot(item, spread, TN)
            r.gates[j, at] = (main * wide).astype(BF)
            r.gates[2 + j, at] = (rest * wide).astype(BF)

    back1 = leave(1)
    for c in sums:
        for copy in c.sib + [c.off_r, c.off_l, c.r0, c.r1, c.l0, c.l1]:
            copy.wait_send()

    def gated(pt, lhs):
        out = []
        for g in range(3):
            value = jnp.zeros((lhs.stop - lhs.start, 256), F32)
            rows = r.bmain[pt, :, :, g * 256 : (g + 1) * 256].reshape(256, 256)
            rest = r.brest[pt].reshape(256, 256)
            mask = iota((lhs.stop - lhs.start, 256), 1) % MAIN // 4 == g
            for j in range(2):
                value = value + dot(r.gates[j, lhs], rows)
                value = value + dot(jnp.where(mask, r.gates[2 + j, lhs], jnp.zeros((), BF)), rest)
            out.append(value)
        return out

    for copy in back0:
        copy.wait()
    primal = gated(0, slice(0, 2 * TOK))
    for g in range(3):
        at = slice(g * 256, (g + 1) * 256)
        r.mixed[:, at] = (r.state[0, :, at].astype(F32) + primal[g][:TOK]).astype(BF)
        r.kept[:, at] = r.state[1, :, at].astype(F32) + primal[g][TOK:]
    for copy in back1:
        copy.wait()
    tangent = gated(1, slice(0, TOK))
    for g in range(3):
        at = slice(g * 256, (g + 1) * 256)
        r.mixed_tan[:, at] = (r.kept[:, at] + tangent[g]).astype(BF)


def shards(
    residual_in, residual_tan, queries, keys, values, query_tan, key_tan, value_tan,
    out_proj, shift_mod, scale_mod, router, up_weight, down_weight, expert_ids,
):
    out = jax.ShapeDtypeStruct((TOK, QUARTER), BF)
    return pl.pallas_call(
        block_kernel,
        out_shape=(out, out),
        in_specs=[pl.BlockSpec(memory_space=pl.ANY)] * 15,
        out_specs=(pl.BlockSpec(memory_space=VMEM),) * 2,
        scratch_shapes=list(SCRATCH.values()),
        compiler_params=pltpu.CompilerParams(
            collective_id=1, has_side_effects=True, vmem_limit_bytes=64 * MIB - 64 * 1024
        ),
        name="block",
    )(
        queries, query_tan, keys, values, key_tan, value_tan, out_proj, residual_in, residual_tan,
        up_weight, down_weight, router.T, shift_mod[None], scale_mod[None], expert_ids.T,
    )


def solution(mesh):
    rows, heads = P("ctx", "exp"), P("exp", None)
    in_specs = (rows,) * 8 + (
        heads, P(), P(), P(), P("ctx", None, "exp"), P("ctx", "exp", None), P("ctx", None),
    )
    return jax.shard_map(shards, mesh=mesh, in_specs=in_specs, out_specs=(rows, rows), check_vma=False)
```

time: 842 us -> 161 us (0.19); the launches traced: 830 us -> 160 us
  waiting for transfers between devices: 541 us -> 0 us
  Pallas kernels: 0 us -> 156 us
  local copies, waits for them, and re-layouts: 97.7 us -> 3.23 us
  matrix products: 77.2 us -> 0 us
  starting transfers between devices: 47.7 us -> 0 us
  other arithmetic: 33.8 us -> 0 us
  blocking collectives: 17.8 us -> 0 us
  between operations: 14.9 us -> 0.65 us
    all_gather x4 -> x0, waiting for transfers between devices: 292 us -> none  [the longest x1 79.9 us: shards(): key_piece = lax.all_gather(keys, 'ctx', axis=0, tiled=True)]
    all_to_all x4 -> x0, waiting for transfers between devices: 174 us -> none  [the longest x1 58.1 us: shards(): lax.all_to_all(packed, 'ctx', split_axis=0, concat_axis=1, tiled=True)]
    pallas_call x0 -> x1, Pallas kernels: none -> 156 us  [shards(): pl.pallas_call(block_kernel, out_shape=(out, out), in_specs=[pl.BlockSpec...]
    dot_general x15 -> x0, matrix products: 77.2 us -> none  [the longest x1 23 us: shards(): jnp.einsum('rmf,rfd->rmd', act_tan.astype(jnp.bfloat16), down_weight, pre...]
    reduce_scatter x4 -> x0, waiting for transfers between devices: 73.2 us -> none  [the longest x1 24.9 us: shards(): lax.psum_scatter(moe_tan.astype(jnp.bfloat16), 'exp', scatter_dimension=1...]
    all_to_all x4 -> x0, starting transfers between devices: 47.1 us -> none  [the longest x1 15.3 us: shards(): lax.all_to_all(packed_tan, 'ctx', split_axis=0, concat_axis=1, tiled=True)]
    reshape x6 -> x0, local copies, waits for them, and re-layouts: 33.7 us -> none  [the longest x2 10.1 us: shards(): folded.reshape(experts * capacity, D)[targets].reshape(tok_rows, 2, D)]
    reduce_sum x8 -> x0, other arithmetic: 27.3 us -> none  [the longest x1 13.8 us: shards(): jnp.sum(gates_tan[:, :, None] * picked + gates[:, :, None] * picked_tan,...]
  transfers between devices with their start and end apart: 12 -> 0, of which waited for: 12 -> 0; matrix products, arithmetic and copies ran while one was open for 12% -> 0% of each run, Pallas kernels for 0% -> 0%
where the time goes in v2:
time: 161 us; the launch traced here: 160 us
  Pallas kernels  156 us (97%)
  local copies, waits for them, and re-layouts  3.23 us (2%)
    pallas_call x1, Pallas kernels, shards(): pl.pallas_call(block_kernel, out_shape=(out, out), in_specs=[pl.BlockSpec...  156 us
    unnamed x2, local copies, waits for them, and re-layouts  3.23 us

profile of v2, /device:TPU:0, one launch (start us, length us, event | category | flops | bytes accessed | tf_op | source)
XLA Modules:
  0.0 160.4 jit_solution(14096204822452595291)
XLA Ops:
  0.6 156.5 %block.1 = (bf16[128,768]{1,0:T(8,128)(2,1)}, bf16[128,768]{1,0:T(8,128)(2,1)}) custom-call(bf16[128,384]{1,0:T(8,128)(2,1)} %refs_0_.1, bf16[128,384]{1,0:T(8,128)(2,1)} %refs_1_.1, bf16[128,384]{1,0:T(8,128)(2,1)} %refs_2_.1, bf16[128,384]{1,0:T(8,128)(2,1)} %refs_3_.1, bf16[128,384]{1,0:T(8,128)(2,1)} %refs_4_.1, bf16[128,384]{1,0:T(8,128)(2,1)} %refs_5_.1, ...), custom_call_target="tpu_custom_call" | custom-call | tf_op jit(solution)/shard_map/block/pallas_call | solution.py:754
  157.1 1.6 %copy.19 = bf16[128,768]{1,0:T(8,128)(2,1)} copy(bf16[128,768]{1,0:T(8,128)(2,1)} %get-tuple-element.4) | data formatting | bytes 393216
  158.8 1.6 %copy.20 = bf16[128,768]{1,0:T(8,128)(2,1)} copy(bf16[128,768]{1,0:T(8,128)(2,1)} %get-tuple-element.5) | data formatting | bytes 393216

commit v3 on v2

--- a/solution.py
+++ b/solution.py
@@ -106,6 +106,7 @@
     "kept": VMEM((TOK, QUARTER), F32),
     "normed": VMEM((2, TOK, QUARTER), BF),
     "gates": VMEM((4, 2 * TOK, 256), BF),
+    "sel": VMEM((4, TOK, 256), BF),
     "pmain": VMEM((2, EXPERTS, MAIN, QUARTER), BF),
     "prest": VMEM((2, EXPERTS, MAIN, 256), BF),
     "zrest": VMEM((2, EXPERTS, MAIN, 256), BF),
@@ -200,23 +201,66 @@
     peers_zy = [device((z + a) % 4, (y + b) % 4, xh, xl, co) for a, b in ZY]
     meet(peers_zy + [near(a, 1) for a in range(4)] + peers_e + [at_pos(other, co)])
 
-    kv = []
-    for n, a in enumerate((1, 3, 2)):
-        peer = device((z + a) % 4, y, xh, xl, co)
-        for i, (src, dst) in enumerate(((r.k, r.kg), (r.kt, r.ktg), (r.v, r.vg), (r.vt, r.vtg))):
-            kv.append(remote(src, dst.at[z], r.kv_s.at[n * 4 + i], r.kv_r.at[n * 4 + i], peer))
-            kv[-1].start()
-
-    def q_copies(a, b):
-        n = 4 * a + 2 * b
-        return [
-            remote(src, dst.at[here_q], r.q_s.at[n + i], r.q_r.at[n + i], near(a, b))
-            for i, (src, dst) in enumerate(((r.q, r.qg), (r.qt, r.qtg)))
+    z_up, z_down = device((z + 1) % 4, y, xh, xl, co), device((z + 3) % 4, y, xh, xl, co)
+    y_up, y_down = near(1, 0), near(3, 0)
+
+    def kv_copy(n, src, dst, at, peer):
+        return remote(src, dst.at[at], r.kv_s.at[n], r.kv_r.at[n], peer)
+
+    kv_pairs = ((r.k, r.kg), (r.kt, r.ktg), (r.v, r.vg), (r.vt, r.vtg))
+    kv_up = [kv_copy(i, src, dst, z, z_up) for i, (src, dst) in enumerate(kv_pairs)]
+    kv_down = [kv_copy(4 + i, src, dst, z, z_down) for i, (src, dst) in enumerate(kv_pairs)]
+    z_before, z_after = (z + 3) % 4, (z + 1) % 4
+    kv_on = [
+        kv_copy(8, r.kg.at[z_before], r.kg, z_before, z_up),
+        kv_copy(9, r.ktg.at[z_before], r.ktg, z_before, z_up),
+        kv_copy(10, r.vg.at[z_after], r.vg, z_after, z_down),
+        kv_copy(11, r.vtg.at[z_after], r.vtg, z_after, z_down),
+    ]
+
+    def q_copy(n, src, dst, at, peer):
+        return remote(src, dst.at[at], r.q_s.at[n], r.q_r.at[n], peer)
+
+    q_pairs = ((r.q, r.qg), (r.qt, r.qtg))
+    q_over = [q_copy(i, src, dst, here_q, near(0, 1)) for i, (src, dst) in enumerate(q_pairs)]
+    there_q = y * 2 + 1 - xh
+
+    def q_round(n, sources, side):
+        mine = y * 2 + side
+        low, high = ((y + 3) % 4) * 2 + side, ((y + 1) % 4) * 2 + side
+        up = [q_copy(n + i, src, dst, mine, y_up) for i, (src, dst) in enumerate(zip(sources, (r.qg, r.qtg)))]
+        down = [q_copy(n + 2 + i, src, dst, mine, y_down) for i, (src, dst) in enumerate(zip(sources, (r.qg, r.qtg)))]
+        on = [
+            q_copy(n + 4, r.qg.at[low], r.qg, low, y_up),
+            q_copy(n + 5, r.qtg.at[high], r.qtg, high, y_down),
         ]
-
-    for a, b in YX:
-        for copy in q_copies(a, b):
+        return up, down, on
+
+    q_own = q_round(2, (r.q, r.qt), xh)
+    q_other = q_round(8, (r.qg.at[there_q], r.qtg.at[there_q]), 1 - xh)
+
+    def start_round(group):
+        up, down, on = group
+        for copy in (up[0], down[1], up[1], down[0]):
             copy.start()
+
+    def pass_round(group):
+        up, down, on = group
+        up[0].wait_recv()
+        on[0].start()
+        down[1].wait_recv()
+        on[1].start()
+
+    for n in (0, 1):
+        q_over[n].start()
+        kv_up[n].start()
+        kv_down[2 + n].start()
+    start_round(q_own)
+    for n in (0, 1):
+        kv_up[2 + n].start()
+        kv_down[n].start()
+    kv = kv_up + kv_down + kv_on
+    queries = q_over + [copy for group in q_own + q_other for copy in group]
     quarter = pl.ds(pl.multiple_of(e * QUARTER, QUARTER), QUARTER)
     local = [
         pltpu.make_async_copy(src, dst, r.lsem.at[i])
@@ -248,13 +292,13 @@
     rank = dot(named, before).astype(BF)
     spread = (iota((EXPERTS, 256), 1) // MAIN == iota((EXPERTS, 256), 0)).astype(BF)
 
-    def selection():
-        named_x = dot(named, spread, TN)
-        rank_x = dot(rank, spread, TN)
-        slot = iota((TOK, 256), 1) % MAIN
-        main = jnp.where(rank_x == slot.astype(F32), named_x, 0.0)
-        rest = jnp.where(rank_x == (MAIN + slot % 4).astype(F32), named_x, 0.0)
-        return main, rest, slot // 4
+    named_x = dot(named, spread, TN)
+    rank_x = dot(rank, spread, TN)
+    slot = iota((TOK, 256), 1) % MAIN
+    r.sel[0] = jnp.where(rank_x == slot.astype(F32), named_x, 0.0).astype(BF)
+    extra = jnp.where(rank_x == (MAIN + slot % 4).astype(F32), named_x, 0.0)
+    for g in range(3):
+        r.sel[1 + g] = jnp.where(slot // 4 == g, extra, 0.0).astype(BF)
 
     def out_copies(a, b, part):
         n = 6 * a + 3 * b
@@ -270,12 +314,23 @@
             )
         return moves
 
+    for copy in q_over:
+        copy.wait_recv()
+    start_round(q_other)
+    for n in (0, 1):
+        kv_up[n].wait_recv()
+        kv_on[n].start()
+        kv_down[2 + n].wait_recv()
+        kv_on[2 + n].start()
+    pass_round(q_own)
+    pass_round(q_other)
     for copy in local[:6]:
         copy.wait()
-    for copy in kv:
+    for copy in kv_up[2:] + kv_down[:2] + kv_on:
         copy.wait_recv()
-    for copy in q_copies(0, 1):
-        copy.wait_recv()
+    for up, down, on in (q_own, q_other):
+        for copy in (up[1], down[0], on[0], on[1]):
+            copy.wait_recv()
     attend(r, y)
     for copy in out_copies(0, 1, 0):
         copy.start()
@@ -289,9 +344,6 @@
 
     def attend_step(i, carry):
         a = 1 + 2 * i - 3 * (i // 2)
-        for b in (0, 1):
-            for copy in q_copies(a, b):
-                copy.wait_recv()
         attend(r, (y + 4 - a) % 4)
         for b in (0, 1):
             for copy in out_copies(4 - a, b, 0):
@@ -303,9 +355,8 @@
         out_copies(a, b, 1)[0].start()
     for copy in kv:
         copy.wait_send()
-    for a, b in YX:
-        for copy in q_copies(a, b):
-            copy.wait_send()
+    for copy in queries:
+        copy.wait_send()
     for copy in local[6:12] + keep:
         copy.wait()
     for a, b in YX:
@@ -387,32 +438,29 @@
     def x_rows_of(pt, source):
         return pl.ds(pl.multiple_of(pt * HALF + (source // 4) * GROUP + (source % 4) * MAIN, MAIN), MAIN)
 
-    def plane(pt, main, rest, send, recv, lsem):
+    def plane(pt, i, src, dst, send, recv, lsem):
         moves = []
-        for i, (src, dst) in enumerate((main, rest)):
-            for n, ((a, b), peer) in enumerate(zip(ZY, peers_zy)):
-                there = ((z + a) % 4) * 4 + (y + b) % 4
-                at = pt * 30 + i * 15 + n
-                moves.append(remote(src(there), dst(here), send.at[at], recv.at[at], peer))
-            moves.append(pltpu.make_async_copy(src(here), dst(here), r.lsem.at[lsem + 2 * pt + i]))
+        for n, ((a, b), peer) in enumerate(zip(ZY, peers_zy)):
+            there = ((z + a) % 4) * 4 + (y + b) % 4
+            at = pt * 30 + i * 15 + n
+            moves.append(remote(src(there), dst(here), send.at[at], recv.at[at], peer))
+        moves.append(pltpu.make_async_copy(src(here), dst(here), r.lsem.at[lsem + 2 * pt + i]))
         for copy in moves:
             copy.start()
         return moves
 
     def route(pt):
-        main, rest, piece = selection()
         rows = r.normed[pt]
-        r.pmain[pt] = dot(main.astype(BF), rows, TN).astype(BF).reshape(EXPERTS, MAIN, QUARTER)
+        r.pmain[pt] = dot(r.sel[0], rows, TN).astype(BF).reshape(EXPERTS, MAIN, QUARTER)
+        moves = plane(
+            pt, 0, lambda s: r.pmain.at[pt, s], lambda s: r.x.at[block, x_rows_of(pt, s)], r.z_s, r.z_r, 15
+        )
         value = jnp.zeros((256, 256), F32)
         for g in range(3):
-            chosen = jnp.where(piece == g, rest, 0.0).astype(BF)
-            value = value + dot(chosen, rows[:, g * 256 : (g + 1) * 256], TN)
+            value = value + dot(r.sel[1 + g], rows[:, g * 256 : (g + 1) * 256], TN)
         r.prest[pt] = value.astype(BF).reshape(EXPERTS, MAIN, 256)
-        return plane(
-            pt,
-            (lambda s: r.pmain.at[pt, s], lambda s: r.x.at[block, x_rows_of(pt, s)]),
-            (lambda s: r.prest.at[pt, s], lambda s: r.zrest.at[pt, s]),
-            r.z_s, r.z_r, 15,
+        return moves + plane(
+            pt, 1, lambda s: r.prest.at[pt, s], lambda s: r.zrest.at[pt, s], r.z_s, r.z_r, 15
         )
 
     def piece_rows(g):
@@ -602,16 +650,16 @@
             return carry
 
         lax.fori_loop(0, 4, step, 0)
+        moves = plane(
+            pt, 0, lambda s: r.total.at[pt, rows_of(s)], lambda s: r.bmain.at[pt, s], r.b_s, r.b_r, 19
+        )
         rest = jnp.concatenate([r.total[pt, i * GROUP + 64 : (i + 1) * GROUP] for i in range(4)], axis=0)
         value = jnp.zeros((256, 256), F32)
         for g in range(3):
             value = value + dot(piece_rows(g), rest[:, g * 256 : (g + 1) * 256], TN)
         r.trest[pt] = value.astype(BF).reshape(EXPERTS, MAIN, 256)
-        return plane(
-            pt,
-            (lambda s: r.total.at[pt, rows_of(s)], lambda s: r.bmain.at[pt, s]),
-            (lambda s: r.trest.at[pt, s], lambda s: r.brest.at[pt, s]),
-            r.b_s, r.b_r, 19,
+        return moves + plane(
+            pt, 1, lambda s: r.trest.at[pt, s], lambda s: r.brest.at[pt, s], r.b_s, r.b_r, 19
         )
 
     merge(0)
@@ -703,7 +751,8 @@
     gate1 = 1.0 / (1.0 + jnp.exp(own0 - own1))
     gates = oh0 * gate0 + oh1 * gate1
     gates_tan = oh0 * (gate0 * (1.0 - gate0) * diff) - oh1 * (gate1 * (1.0 - gate1) * diff)
-    main, rest, piece = selection()
+    main = r.sel[0].astype(F32)
+    rest = (r.sel[1] + r.sel[2] + r.sel[3]).astype(F32)
     for i, g in enumerate((gates, gates_tan)):
         high = g.astype(BF)
         low = (g - high.astype(F32)).astype(BF)

time: 161 us -> 157 us (0.975)
  Pallas kernels: 156 us -> 152 us
    pallas_call x1, Pallas kernels: 156 us -> 152 us  [shards(): pl.pallas_call(block_kernel, out_shape=(out, out), in_specs=[pl.BlockSpec...]
where the time goes in v3:
time: 157 us; the launch traced here: 156 us
  Pallas kernels  152 us (97%)
  local copies, waits for them, and re-layouts  3.23 us (2%)
    pallas_call x1, Pallas kernels, shards(): pl.pallas_call(block_kernel, out_shape=(out, out), in_specs=[pl.BlockSpec...  152 us
    unnamed x2, local copies, waits for them, and re-layouts  3.23 us

profile of v3, /device:TPU:0, one launch (start us, length us, event | category | flops | bytes accessed | tf_op | source)
XLA Modules:
  0.0 156.3 jit_solution(17020172984566986374)
XLA Ops:
  0.6 152.4 %block.1 = (bf16[128,768]{1,0:T(8,128)(2,1)}, bf16[128,768]{1,0:T(8,128)(2,1)}) custom-call(bf16[128,384]{1,0:T(8,128)(2,1)} %refs_0_.1, bf16[128,384]{1,0:T(8,128)(2,1)} %refs_1_.1, bf16[128,384]{1,0:T(8,128)(2,1)} %refs_2_.1, bf16[128,384]{1,0:T(8,128)(2,1)} %refs_3_.1, bf16[128,384]{1,0:T(8,128)(2,1)} %refs_4_.1, bf16[128,384]{1,0:T(8,128)(2,1)} %refs_5_.1, ...), custom_call_target="tpu_custom_call" | custom-call | tf_op jit(solution)/shard_map/block/pallas_call | solution.py:803
  153.1 1.6 %copy.19 = bf16[128,768]{1,0:T(8,128)(2,1)} copy(bf16[128,768]{1,0:T(8,128)(2,1)} %get-tuple-element.4) | data formatting | bytes 393216
  154.7 1.6 %copy.20 = bf16[128,768]{1,0:T(8,128)(2,1)} copy(bf16[128,768]{1,0:T(8,128)(2,1)} %get-tuple-element.5) | data formatting | bytes 393216

commit v4 on v3

--- a/solution.py
+++ b/solution.py
@@ -676,10 +676,10 @@
         out_copies(a, b, 1)[0].wait()
     merge(1)
     start_projection(1)
+    end_projection(1)
+    moves = start_mean(1)
     end_route(0, route0)
     start_ring(0)
-    end_projection(1)
-    moves = start_mean(1)
     cross = end_mean(1, moves)
     sf, tf = r.state[0].astype(F32), r.state[1].astype(F32)
     r.normed[1] = ((tf * recip - sf * (recip * recip * recip) * cross) * gain).astype(BF)

time: 157 us -> 153 us (0.975)
  Pallas kernels: 152 us -> 149 us
    pallas_call x1, Pallas kernels: 152 us -> 149 us  [shards(): pl.pallas_call(block_kernel, out_shape=(out, out), in_specs=[pl.BlockSpec...]
where the time goes in v4:
time: 153 us
  Pallas kernels  149 us (97%)
  local copies, waits for them, and re-layouts  3.23 us (2%)
    pallas_call x1, Pallas kernels, shards(): pl.pallas_call(block_kernel, out_shape=(out, out), in_specs=[pl.BlockSpec...  149 us
    unnamed x2, local copies, waits for them, and re-layouts  3.23 us

profile of v4, /device:TPU:0, one launch (start us, length us, event | category | flops | bytes accessed | tf_op | source)
XLA Modules:
  0.0 152.7 jit_solution(3841390237425315674)
XLA Ops:
  0.6 148.9 %block.1 = (bf16[128,768]{1,0:T(8,128)(2,1)}, bf16[128,768]{1,0:T(8,128)(2,1)}) custom-call(bf16[128,384]{1,0:T(8,128)(2,1)} %refs_0_.1, bf16[128,384]{1,0:T(8,128)(2,1)} %refs_1_.1, bf16[128,384]{1,0:T(8,128)(2,1)} %refs_2_.1, bf16[128,384]{1,0:T(8,128)(2,1)} %refs_3_.1, bf16[128,384]{1,0:T(8,128)(2,1)} %refs_4_.1, bf16[128,384]{1,0:T(8,128)(2,1)} %refs_5_.1, ...), custom_call_target="tpu_custom_call" | custom-call | tf_op jit(solution)/shard_map/block/pallas_call | solution.py:803
  149.5 1.6 %copy.19 = bf16[128,768]{1,0:T(8,128)(2,1)} copy(bf16[128,768]{1,0:T(8,128)(2,1)} %get-tuple-element.4) | data formatting | bytes 393216
  151.1 1.6 %copy.20 = bf16[128,768]{1,0:T(8,128)(2,1)} copy(bf16[128,768]{1,0:T(8,128)(2,1)} %get-tuple-element.5) | data formatting | bytes 393216
